TPU v7x, 128 devices: a whole 4x4x4 slice. The times are simulated.
128 devices in a mesh: row: 16 (over z_lo, y, core), col: 8 (over x, z_hi).
Axes of the slice: x: 4, y: 4, z: 4 (z_hi: 2, z_lo: 2; z = z_hi * 2 + z_lo), core: 2. Of those that a mesh axis runs over, the one named last changes fastest.
Arguments:
- weights: bfloat16 [32768, 1024], P(('row', 'col')), may hold values from -6 to 6
- tile_pattern: int32 [128, 2], P(('row', 'col')), may hold values 0 or 1
Outputs:
- similarity: bfloat16 [32768, 32768], P('row', 'col')
Inputs may be any that keep to these rules, and one draw needn't show every extreme that they name: `tile_pattern`: 1 where the tile holds weights, 0 where it is empty.
All inputs are finite; a program needn't handle non-finite values. No bound on the sum of `tile_pattern` on one device may be relied on, other than what follows from the above.
Results may differ from a plain program's by a relative error of at most 0.001.
Values may be sent and summed in bfloat16 or wider, within the bound.
A program may use at most 128 MiB of HBM per device.

v0:
```python
import math

import jax
import jax.numpy as jnp
from jax import lax
from jax.sharding import PartitionSpec as P


def from_root(value, axis, source):
    kept = jnp.where(lax.axis_index(axis) == source, value, 0).astype(value.dtype)
    return lax.psum(kept, axis)


def shards(weights, tile_pattern):
    reads_dev = weights.shape[0]
    section_count = tile_pattern.shape[1]
    tile_rows = reads_dev // tile_pattern.shape[0]
    bin_tile = weights.shape[1] // section_count
    tile_mask = jnp.repeat(tile_pattern, tile_rows, axis=0).astype(jnp.bfloat16)
    masked = (weights.reshape(reads_dev, section_count, bin_tile) * tile_mask[:, :, None]).reshape(
        reads_dev, section_count * bin_tile
    )
    col_count = lax.axis_size("col")
    row_count = lax.axis_size("row")
    owner_rows = row_count // col_count
    row_block = reads_dev * col_count
    col_block = reads_dev * row_count
    col_index = lax.axis_index("col")
    row_index = lax.axis_index("row")
    scale = 1.0 / math.sqrt(section_count * bin_tile)
    row_ids = row_index * row_block + jnp.arange(row_block, dtype=jnp.int32)
    local_cols = jnp.arange(row_block, dtype=jnp.int32)

    def column_slot(member):
        return member + 0 * col_index

    slot_list = [column_slot(member) for member in range(owner_rows)]
    blocks = []
    left_parts = []
    right_parts = [[] for member in range(owner_rows)]
    for section_idx in range(section_count):
        panel_rows = masked[:, section_idx * bin_tile : (section_idx + 1) * bin_tile]
        left_piece = lax.all_gather(panel_rows, "col", axis=0, tiled=True)
        left_parts.append(left_piece)
        for member in range(owner_rows):
            right_piece = from_root(left_piece, "row", owner_rows * col_index + slot_list[member])
            right_parts[member].append(right_piece)
    left_side = jnp.concatenate(left_parts, axis=1)
    for member in range(owner_rows):
        right_side = jnp.concatenate(right_parts[member], axis=1)
        product = lax.dot_general(
            left_side, right_side, (((1,), (1,)), ((), ())), preferred_element_type=jnp.float32
        )
        col_ids = col_index * col_block + slot_list[member] * row_block + local_cols
        same = row_ids[:, None] == col_ids[None, :]
        blocks.append(
            jnp.where(same, jnp.float32(0.0), product * jnp.float32(scale)).astype(jnp.bfloat16)
        )
    stacked = jnp.stack(blocks, axis=0)
    return jnp.transpose(stacked, (1, 0, 2)).reshape(row_block, col_block)


def solution(mesh):
    return jax.shard_map(
        shards,
        mesh=mesh,
        in_specs=(P(("row", "col"), None), P(("row", "col"), None)),
        out_specs=P("row", "col"),
        check_vma=False,
    )
```

profile of v0, /device:TPU:7, one launch (start us, length us, event | category | flops | bytes accessed | tf_op | source)
XLA Modules:
  0.0 326.3 jit_solution(13519848451069507380)
XLA Ops:
  6.5 0.0 all-gather.3.cloned.1.call-start
  6.5 0.7 convert_bitcast_fusion
  7.2 0.1 broadcast_bitcast_fusion
  7.3 1.1 broadcast_multiply_fusion
  8.4 0.8 fusion.10
  9.2 0.0 all-gather.3.cloned.1.call-update
  9.2 0.0 all-gather.5.cloned.1.call-start
  9.3 0.7 all-gather.5.cloned.1.call-update
  10.0 0.0 all-reduce.3.cloned.1.call-start
  10.0 54.8 %all-gather.3.cloned.1.call-done = bf16[2048,512]{1,0:T(8,128)(2,1)} async-done(((bf16[256,512]{1,0:T(8,128)(2,1)}), bf16[2048,512]{1,0:T(8,128)(2,1)}) %all-gather.3.cloned.1.call-update) | async-done | bytes 2097168 | tf_op jit(solution)/shard_map/all_gather | solution.py:43
  64.8 4.9 %broadcast_select_fusion.3 = (bf16[2048,512]{1,0:T(8,128)(2,1)}, bf16[2048,512]{1,0:T(8,128)(2,1)}, bf16[2048,1024]{1,0:T(8,128)(2,1)}) fusion(bf16[2048,512]{1,0:T(8,128)(2,1)} %all-gather.3.cloned.1.call-done, pred[]{:T(512)S(6)} %eq.17, pred[]{:T(512)S(6)} %eq.38), kind=kLoop, calls=%fused_computation.14 | loop fusion | flops 2097151 | bytes 8388610 | tf_op jit(solution)/shard_map/jit(_where)/select_n | solution.py:10
  69.7 51.1 %all-gather.5.cloned.1.call-done = bf16[2048,512]{1,0:T(8,128)(2,1)} async-done(((bf16[256,512]{1,0:T(8,128)(2,1)}), bf16[2048,512]{1,0:T(8,128)(2,1)}) %all-gather.5.cloned.1.call-update) | async-done | bytes 2097168 | tf_op jit(solution)/shard_map/all_gather | solution.py:43
  120.8 5.5 %broadcast_select_fusion.2 = (bf16[2048,512]{1,0:T(8,128)(2,1)}, bf16[2048,512]{1,0:T(8,128)(2,1)}, bf16[2048,1024]{1,0:T(8,128)(2,1)}) fusion(bf16[2048,512]{1,0:T(8,128)(2,1)} %all-gather.5.cloned.1.call-done, pred[]{:T(512)S(6)} %eq.17, pred[]{:T(512)S(6)} %eq.38, bf16[2048,1024]{1,0:T(8,128)(2,1)} %get-tuple-element.11), kind=kLoop, calls=%fused_computation.13 | loop fusion | flops 2097152 | bytes 8388610 | tf_op jit(solution)/shard_map/jit(_where)/select_n | solution.py:10
  126.4 0.0 all-reduce.3.cloned.1.call-update
  126.4 142.8 %all-reduce.3.cloned.1.call-done = (bf16[2048,512]{1,0:T(8,128)(2,1)}, bf16[2048,512]{1,0:T(8,128)(2,1)}, bf16[2048,512]{1,0:T(8,128)(2,1)}, bf16[2048,512]{1,0:T(8,128)(2,1)}) async-done(((bf16[2048,512]{1,0:T(8,128)(2,1)}, bf16[2048,512]{1,0:T(8,128)(2,1)}, bf16[2048,512]{1,0:T(8,128)(2,1)}, bf16[2048,512]{1,0:T(8,128)(2,1)}), (bf16[2048,512]{1,0:T(8,128)(2,1)}, bf16[2048,512]{1,0:T(8,128)(2,1)}, ...) | async-done | bytes 8388624 | tf_op jit(solution)/shard_map/psum | solution.py:11
  269.2 0.0 copy-start
  269.2 0.0 copy-start.1
  269.2 12.1 %fusion.1 = bf16[1,2048,2048]{1,2,0:T(8,128)(2,1)S(1)} fusion(bf16[2048,1024]{1,0:T(8,128)(2,1)} %get-tuple-element.14, s32[2048]{0:T(1024)S(1)} %get-tuple-element.17, s32[2048]{0:T(1024)S(1)} %get-tuple-element.18, bf16[2048,512]{1,0:T(8,128)(2,1)} %get-tuple-element.5, bf16[2048,512]{1,0:T(8,128)(2,1)} %get-tuple-element.6), kind=kOutput, calls=%fused_computation.4 | convolution fusion | flops 8615100416 | bytes 16793600 | tf_op jit(solution)/shard_map/dot_general | solution.py:51
  281.3 0.0 copy-done
  281.3 0.0 copy-done.1
  281.3 10.4 %fusion = bf16[1,2048,2048]{1,2,0:T(8,128)(2,1)S(1)} fusion(bf16[2048,1024]{1,0:T(8,128)(2,1)S(1)} %copy-done, s32[2048]{0:T(1024)S(1)} %iota_add_fusion.1, s32[2048]{0:T(1024)S(1)} %get-tuple-element.18, bf16[2048,512]{1,0:T(8,128)(2,1)S(1)} %copy-done.1, bf16[2048,512]{1,0:T(8,128)(2,1)} %get-tuple-element.8), kind=kOutput, calls=%fused_computation.3 | convolution fusion | flops 8615100416 | bytes 16793600 | tf_op jit(solution)/shard_map/dot_general | solution.py:51
  291.7 6.8 %pad_maximum_fusion = bf16[2,2048,2048]{1,2,0:T(8,128)(2,1)} fusion(bf16[1,2048,2048]{1,2,0:T(8,128)(2,1)S(1)} %fusion.1, bf16[1,2048,2048]{1,2,0:T(8,128)(2,1)S(1)} %fusion), kind=kLoop, calls=%fused_computation | loop fusion | flops 8388608 | bytes 33554432 | tf_op jit(solution)/shard_map/stack | solution.py:59
  298.6 21.2 %copy.3 = bf16[2048,4096]{1,0:T(8,128)(2,1)} copy(bf16[2048,4096]{0,1:T(8,128)(2,1)} %bitcast.14) | data formatting | bytes 33554432 | tf_op jit(solution)/shard_map/reshape | solution.py:60
  (3 shorter events, 0.0 us)
Async XLA Ops:
  6.5 58.3 %all-gather.3.cloned.1.call-start = ((), (), s32[]{:S(2)}) async-start(), calls=%async_computation | async-start | bytes 2359296 | tf_op jit(solution)/shard_map/all_gather | solution.py:43
  9.2 111.6 %all-gather.5.cloned.1.call-start = ((), (), s32[]{:S(2)}) async-start(), calls=%async_computation.1 | async-start | bytes 2359296 | tf_op jit(solution)/shard_map/all_gather | solution.py:43
  10.0 259.2 %all-reduce.3.cloned.1.call-start = ((), (), s32[]{:S(2)}) async-start(), calls=%async_computation.2 | async-start | bytes 16777216 | tf_op jit(solution)/shard_map/psum | solution.py:11
  269.2 12.1 %copy-start = (bf16[2048,1024]{1,0:T(8,128)(2,1)S(1)}, bf16[2048,1024]{1,0:T(8,128)(2,1)}, u32[]{:S(2)}) copy-start(bf16[2048,1024]{1,0:T(8,128)(2,1)} %get-tuple-element.14) | copy-start | bytes 12582916
  269.2 12.1 %copy-start.1 = (bf16[2048,512]{1,0:T(8,128)(2,1)S(1)}, bf16[2048,512]{1,0:T(8,128)(2,1)}, u32[]{:S(2)}) copy-start(bf16[2048,512]{1,0:T(8,128)(2,1)} %get-tuple-element.7) | copy-start | bytes 6291460
Sparse Core Ops, SparseCore 0:
  9.7 55.1 all-gather.2
  67.2 53.6 all-gather.4
  126.5 142.6 all-reduce.2
where the time goes:
time: 329 us; the launch traced here: 326 us
  waiting for transfers between devices  249 us (76%)
  matrix products  22.5 us (7%)
  local copies, waits for them, and re-layouts  22.1 us (7%)
  other arithmetic  19 us (6%)
  between operations  13.2 us (4%)
    psum x1, waiting for transfers between devices, from_root(): return lax.psum(kept, axis)  143 us
    all_gather x2, waiting for transfers between devices, shards(): left_piece = lax.all_gather(panel_rows, 'col', axis=0, tiled=True)  106 us
    dot_general x2, matrix products, shards(): lax.dot_general(left_side, right_side, (((1,), (1,)), ((), ())), preferre...  22.5 us
    reshape x1, local copies, waits for them, and re-layouts, shards(): return jnp.transpose(stacked, (1, 0, 2)).reshape(row_block, col_block)  21.2 us
    select_n x2, other arithmetic, from_root(): jnp.where(lax.axis_index(axis) == source, value, 0).astype(value.dtype)  10.4 us
    another operation x1, other arithmetic, shards(): stacked = jnp.stack(blocks, axis=0)  6.82 us
  transfers between devices with their start and end apart: 3, of which 3 were waited for; matrix products, arithmetic and copies ran while one was open for 1% of the time, Pallas kernels for 0%

commit v1 on v0

v1 whole, which is shorter than its diff:
```python
import math

import jax
import jax.numpy as jnp
from jax import lax
from jax.experimental import pallas as pl
from jax.experimental.pallas import tpu as pltpu
from jax.sharding import PartitionSpec as P

MESH = pl.DeviceIdType.MESH
CHUNKS = 4
SLOTS = (
    (
        (0,0,((0,0,1,2,3,6),(0,1,0,1,5,6),(0,2,0,1,4,6),(0,3,0,2,3,6))),
        (0,1,((1,0,1),(1,1,0,1),(1,2,0,1,2),(1,3,0,1))),
        (0,2,((2,0,1),(2,1,0,1,2),(2,2,0,1),(2,3,0,1,2))),
        (0,3,((3,0,2),(3,1,0,1,2),(3,2,0,1,2),(3,3,0,1))),
        (0,4,((4,0,1,2),(4,1,0,2),(4,2,0,1,2),(4,3,1))),
        (0,5,((5,0,1,2),(5,1,0),(5,2,0,1,2),(5,3,0,2))),
        (0,6,((6,0,0,2),(6,1,0,2),(6,2,0,1),(6,3,1))),
        (0,7,((7,0,0,1),(7,1,0,1),(7,2,0,1),(7,3,0,1,2))),
    ),
    (
        (0,0,((1,0,1,2,5,6),(3,1,4,6))),
        (0,1,((0,1,2),(2,0,1,2))),
        (0,2,((1,1,0,2),(3,1,2))),
        (0,3,((0,0),(2,1))),
        (0,4,((5,0,1,2),(7,0,2))),
        (0,5,((4,1,0,2),(6,2,2))),
        (0,6,((5,1,2),(7,0,2))),
        (0,7,((4,0),(6,0))),
        (1,1,((0,0,3,5,6),)),
        (1,3,((0,2,4,5,6),)),
    ),
    (
        (0,0,((4,0,0,3,6),)),
        (0,1,((5,0),)),
        (0,2,((6,0,0),)),
        (0,3,((7,3,0),)),
        (0,4,((0,0,0),)),
        (0,5,((1,2,0),)),
        (0,6,((2,1,0,1),)),
        (0,7,((3,0,0,1),)),
        (1,4,((0,1,3,4,6),)),
    ),
    (
        (0,0,((1,1,2,4,6),(3,2,0,5,6))),
        (0,1,((0,2,0,2),(2,1))),
        (0,2,((1,2,0),(3,2))),
        (0,3,((0,1,1,2),(2,2,0))),
        (0,4,((5,2),(7,1))),
        (0,5,((4,2),(6,3,1,2))),
        (0,6,((5,2,0,2),(7,1,1,2))),
        (0,7,((4,2),(6,1,2))),
        (1,1,((0,3,3,6),)),
    ),
    (
        (0,0,((4,1,1,3,6),)),
        (0,1,((5,2,1),)),
        (0,2,((6,1,1),)),
        (0,4,((0,3),)),
        (0,6,((2,3,1),)),
        (0,7,((3,1),)),
        (1,2,((0,0,3,6),(0,2,4,5,6))),
        (1,3,((3,1,4,5,6),)),
    ),
    (
        (0,0,((1,2,3,6),(3,3,2,4,6))),
        (0,1,((0,3,0),(2,2,2))),
        (0,2,((1,3),(3,3,2))),
        (0,3,((0,2),(2,3,2))),
        (0,4,((7,2,2),)),
        (0,5,((0,0,2,0),(2,0,0,1),(2,1))),
        (0,6,((5,3,0),(7,2,1))),
        (0,7,((4,3,1,2),(6,2,0))),
        (1,1,((4,0,3,5,6),)),
        (1,4,((1,0,3,4,6),)),
        (1,5,((0,0,4,6),(0,1,5,6))),
        (1,7,((0,1,5,4,6),(0,2,3,6))),
    ),
    (
        (0,0,((4,2,1,5,6),)),
        (0,1,((5,3,1),)),
        (0,2,((7,0),)),
        (0,4,((1,0,0),(6,3,1))),
        (0,6,((1,1),)),
        (0,7,((3,2,0,1),)),
        (1,2,((0,3,5,6),)),
        (1,3,((1,1,4,5,6),)),
    ),
    (
        (0,0,((1,3,2,5,6),(7,3,4,6))),
        (0,1,((2,3,1),(4,0,0))),
        (0,2,((0,1),(0,2,2))),
        (0,3,((1,0,1,2),(1,1,2),(6,1,0))),
        (0,4,((7,3,0),)),
        (0,5,((7,1),(0,1,1,0))),
        (0,6,((4,1,0),(7,3,2))),
        (0,7,((2,1,0),(5,0,2))),
        (1,1,((4,1,3,5,6),)),
    ),
    (
        (0,0,((5,0,3,6),)),
        (0,1,((4,1),)),
        (0,2,((5,1,0),)),
        (0,4,((1,1,0),)),
        (0,6,((3,1,1),)),
        (0,7,((0,1),)),
        (1,1,((0,2,6),)),
        (1,2,((3,1,4,6),)),
        (1,3,((0,0,6),)),
        (1,4,((3,2,3,4,6),(0,0,4,6),(0,2,6))),
        (1,5,((1,0,5,3,6),)),
        (1,6,((0,1,5,6),(0,2,4,6))),
        (1,7,((1,0,5,6),(3,1,3,4,6))),
    ),
    (
        (0,0,((2,0,1,3,6),(2,2,4,6))),
        (0,1,((3,2,2),(6,1,2))),
        (0,2,((0,3,0,2),)),
        (0,3,((4,1,1),(6,0,0))),
        (0,4,((2,0,1),(3,0,2,0))),
        (0,5,((2,3,1),)),
        (0,6,((1,2),(3,0,2))),
        (0,7,((5,2,2),)),
        (1,1,((0,1,6),)),
        (1,2,((4,0,3,5,6),)),
        (1,3,((3,3,4,5,6),(0,1,6))),
        (1,5,((4,0,4,6),)),
    ),
    (
        (0,3,((4,3,0),)),
        (0,5,((0,2,1),(1,0,0))),
        (0,7,((6,3),)),
        (1,1,((1,2,3,5,6),)),
        (1,2,((1,1,4,6),)),
    ),
    (
        (0,0,((7,0,1,0,5,6),)),
        (0,1,((6,2,0),)),
        (0,2,((1,0),(7,1,1))),
        (0,4,((3,3,1),(0,1))),
        (0,6,((3,3,1),)),
        (0,7,((2,3),)),
        (1,2,((4,1,3,6),)),
        (1,3,((7,3,4,6),)),
        (1,4,((4,2,3,4,6),)),
        (1,5,((3,2,5,3,6),)),
        (1,6,((0,3,4,3,6),)),
        (1,7,((1,1,3,4,6),(3,2,6))),
    ),
    (
        (0,0,((5,2,3,6),(6,1,2,4,6))),
        (0,2,((4,0,2,0),)),
        (0,3,((1,2,2),(4,2,1),(5,0,1))),
        (0,4,((6,2,2),)),
        (0,5,((7,2,2),(7,3),(2,2,0,1))),
        (0,6,((2,0),(4,3,1))),
        (0,7,((5,3,0),(2,0))),
        (1,1,((3,1,6),(5,0,3,5,6))),
        (1,2,((3,3,4,6),)),
        (1,3,((4,0,6),)),
        (1,4,((3,1,6),)),
        (1,5,((4,1,4,3,6),(0,2,6))),
        (1,6,((1,0,5,6),(3,1,4,6))),
    ),
    (
        (0,0,((7,2,1,5,6),)),
        (0,1,((6,3,0,1),)),
        (0,2,((4,1),(5,2))),
        (0,4,((2,3),(1,3,1))),
        (0,6,((0,2),)),
        (0,7,((1,0),)),
        (1,1,((1,0,6),)),
        (1,2,((0,1,6),(1,2,3,6))),
        (1,3,((1,0,6),(2,2,4,5,6))),
        (1,4,((4,0,6),(1,3,3,4,6))),
    ),
    (
        (0,0,((5,3,1,3,6),(6,0,2,0,4,6))),
        (0,3,((2,0),(5,1,2,0),(5,2))),
        (0,4,((3,2),)),
        (0,5,((3,1,2,1),(1,1))),
        (0,6,((0,0,2,0),(3,2))),
        (0,7,((4,1),)),
        (1,1,((1,1,6),(2,0,3,6))),
        (1,5,((4,2,5,3,6),)),
        (1,6,((4,0,3,6),)),
        (1,7,((0,0,4,6),(3,3,3,4,6))),
    ),
    (
        (0,1,((7,0,2),(7,1,1))),
        (0,2,((6,2,0),(4,2,2,1))),
        (0,5,((3,2),)),
        (0,7,((3,3),)),
        (1,2,((7,3,4,5,6),)),
        (1,3,((4,1,6),(6,1,4,5,6))),
        (1,4,((1,1,6),)),
        (1,5,((1,2,4,3,6),(0,3,4,6))),
        (1,6,((1,1,4,6),(3,2,5,6))),
        (1,7,((0,3,5,6),)),
    ),
    (
        (0,0,((3,0,3,6),(2,3,5,6),(4,3,0,4,6))),
        (0,1,((0,0),)),
        (0,2,((7,3,1),)),
        (0,3,((0,3,2),(7,0))),
        (0,4,((0,2,1),(2,1,2),(6,1))),
        (0,5,((3,3,2),)),
        (0,6,((0,3,1),(0,1))),
        (0,7,((1,1),)),
        (1,1,((3,2,6),(3,3,6))),
        (1,2,((5,0,3,6),)),
        (1,4,((4,1,6),(7,0,3,4,6))),
        (1,7,((4,2,6),)),
    ),
    (
        (0,2,((6,3,0),)),
        (0,5,((3,0),(6,1))),
        (0,7,((1,3,2,1),)),
        (1,1,((5,2,3,5,6),)),
        (1,2,((1,0,6),(2,2,4,6))),
        (1,3,((1,2,6),)),
        (1,5,((1,3,5,6),(3,1,6))),
        (1,6,((0,0,6),(4,1,3,6))),
        (1,7,((2,2,3,4,6),)),
    ),
    (
        (0,0,((5,1,2,0,4,6),(6,3,3,5,6),(6,2,4,5,6))),
        (0,1,((6,0),(7,2,0))),
        (0,2,((5,0,2),(3,0,1))),
        (0,3,((4,0),(7,2))),
        (0,4,((2,2),(5,3))),
        (0,5,((4,3),)),
        (0,6,((1,0),(4,0,1))),
        (0,7,((0,0),(1,2,0))),
        (1,1,((7,3,6),)),
        (1,2,((2,0,5,6),)),
        (1,3,((6,0,4,5,6),)),
        (1,4,((3,3,6),)),
        (1,5,((5,0,4,3,6),)),
        (1,7,((4,0,6),(1,3,5,4,6))),
    ),
    (
        (0,1,((4,2),)),
        (0,4,((6,0,0),)),
        (0,7,((0,2),)),
        (1,1,((4,2,6),(5,3,3,5,6))),
        (1,2,((6,1,4,6),)),
        (1,4,((1,2,6),(7,2,3,4,6))),
        (1,6,((7,3,4,3,6),)),
    ),
    (
        (0,1,((4,3,0),)),
        (0,4,((3,1),)),
        (0,5,((7,0),)),
        (1,2,((3,2,3,6),(5,2,3,5,6))),
        (1,3,((0,3,6),(5,0,6),(4,3,4,5,6))),
        (1,5,((1,1,6),(7,0,5,3,6))),
        (1,6,((3,3,4,6),(4,2,5,6))),
        (1,7,((6,1,3,4,6),(7,0,5,6))),
    ),
    (
        (0,0,((7,1,1,4,5,6),(2,1,3,4,5,6))),
        (0,1,((3,1),(7,3))),
        (0,2,((0,0),)),
        (0,3,((5,3,1),(6,2))),
        (0,5,((0,3),)),
        (0,6,((2,2,0),(4,2),(1,3,1))),
        (0,7,((5,1),)),
        (1,1,((2,2,6),(3,0,3,5,6))),
        (1,2,((6,0,4,6),)),
        (1,4,((0,3,6),(2,2,6))),
        (1,5,((5,2,4,6),)),
        (1,7,((4,1,6),)),
    ),
    (
        (0,1,((5,1),)),
        (0,2,((7,2),)),
        (0,3,((1,3),)),
        (0,4,((1,2),)),
        (0,5,((6,0),)),
        (1,1,((1,3,6),)),
        (1,3,((5,1,4,5,6),)),
        (1,4,((2,3,3,4,6),)),
        (1,6,((1,2,3,6),(2,2,4,6))),
    ),
    (
        (0,1,((3,3),)),
        (0,3,((6,3),)),
        (0,4,((5,1),)),
        (0,5,((4,0),)),
        (0,6,((5,0),)),
        (0,7,((0,3),)),
        (1,1,((6,1,6),(6,3,3,6))),
        (1,2,((5,3,3,6),)),
        (1,3,((1,3,6),(3,2,6))),
        (1,4,((5,0,6),)),
        (1,5,((7,3,6),(7,2,5,3,6))),
        (1,6,((2,0,4,3,6),)),
        (1,7,((7,2,5,6),(6,0,3,4,6),(7,3,3,6))),
    ),
    (
        (0,1,((3,0),)),
        (0,2,((5,3),(4,3))),
        (0,3,((7,1),)),
        (0,7,((2,2),)),
        (1,2,((4,3,4,6),(4,2,3,6))),
        (1,3,((6,2,4,6),)),
        (1,4,((6,1,3,6),)),
        (1,5,((5,3,4,3,6),)),
        (1,6,((1,3,5,6),(5,0,3,6))),
    ),
    (
        (0,5,((1,3),)),
        (1,1,((7,0,6),(6,0,6))),
        (1,2,((3,0,3,5,6),)),
        (1,3,((7,0,6),)),
        (1,4,((6,3,3,4,6),)),
        (1,5,((3,3,6),)),
    ),
    (
        (1,1,((2,1,5,6),)),
        (1,2,((5,1,4,6),)),
        (1,3,((5,2,6),)),
        (1,4,((5,2,6),)),
        (1,5,((2,3,5,3,6),)),
        (1,6,((5,2,3,6),(6,1,6),(7,0,5,6))),
        (1,7,((1,2,6),(2,3,5,6),(4,3,3,4,6))),
    ),
    (
        (1,1,((4,3,6),(7,2,6))),
        (1,2,((6,3,3,6),)),
        (1,3,((7,1,4,5,6),)),
        (1,4,((6,0,6),)),
        (1,5,((3,0,4,6),(2,2,6))),
    ),
    (
        (1,2,((6,2,4,5,6),)),
        (1,3,((5,3,6),(7,2,6))),
        (1,4,((5,3,4,6),(6,2,3,4,6))),
        (1,5,((6,1,6),)),
        (1,7,((2,0,5,6),)),
    ),
    (
        (1,2,((1,3,6),)),
        (1,3,((2,1,4,5,6),)),
        (1,4,((7,3,6),)),
        (1,5,((2,0,4,6),)),
        (1,6,((6,0,4,6),(7,2,5,6),(3,0,3,6))),
        (1,7,((6,3,4,6),(5,1,3,4,6))),
    ),
    (
        (1,1,((5,1,5,6),(2,3,6))),
        (1,2,((7,1,4,5,6),)),
        (1,3,((4,2,6),)),
        (1,5,((2,1,3,6),(6,3,6))),
        (1,7,((5,0,6),)),
    ),
    (
        (1,2,((7,0,6),)),
        (1,3,((2,3,4,6),)),
        (1,4,((3,0,6),(7,1,3,6))),
        (1,6,((4,3,4,6),(5,3,6))),
    ),
    (
        (1,1,((6,2,6),)),
        (1,3,((3,0,6),)),
        (1,4,((4,3,6),)),
        (1,5,((6,0,6),)),
        (1,6,((6,2,6),)),
        (1,7,((5,3,6),(7,1,6),(5,2,6))),
    ),
    (
        (1,2,((2,1,6),)),
        (1,4,((2,0,6),)),
        (1,5,((6,2,6),)),
        (1,6,((2,3,6),(6,3,6))),
    ),
    (
        (1,1,((7,1,6),)),
        (1,2,((7,2,6),)),
        (1,3,((2,0,6),)),
        (1,4,((5,1,6),(2,1,6))),
        (1,5,((5,1,6),)),
        (1,7,((6,2,6),)),
    ),
    (
        (1,2,((2,3,6),)),
        (1,3,((6,3,6),)),
        (1,5,((4,3,6),(7,1,6))),
        (1,6,((2,1,6),(5,1,6),(7,1,6))),
        (1,7,((3,0,6),(2,1,6))),
    ),
)
XP, XM, ZH, YP, YM, ZL, CORE = range(7)


def place():
    row, col = lax.axis_index("row"), lax.axis_index("col")
    return col // 2, lax.rem(col, 2), lax.rem(row // 2, 4), row // 8, lax.rem(row, 2)


def device(x, zh, y, zl, core):
    return (zl * 8 + y * 2 + core, x * 2 + zh)


def neighbours(x, zh, y, zl, core):
    def turn(a, by):
        return lax.rem(a + by, 4)

    return {
        XP: device(turn(x, 1), zh, y, zl, core),
        XM: device(turn(x, 3), zh, y, zl, core),
        ZH: device(x, 1 - zh, y, zl, core),
        YP: device(x, zh, turn(y, 1), zl, core),
        YM: device(x, zh, turn(y, 3), zl, core),
        ZL: device(x, zh, y, 1 - zl, core),
        CORE: device(x, zh, y, zl, 1 - core),
    }


def flip(a, b):
    return a + b - 2 * a * b


def gather_kernel(pattern_ref, weights_ref, left, right, send_sems, row_sems, col_sems, core_sem, local_sem):
    reads, bins = weights_ref.shape
    section_count = pattern_ref.shape[1]
    bin_tile = bins // section_count
    piece = reads // CHUNKS
    x, zh, y, zl, core = place()
    near = neighbours(x, zh, y, zl, core)
    barrier = pltpu.get_barrier_semaphore()
    for target in near.values():
        pl.semaphore_signal(barrier, inc=1, device_id=target, device_id_type=MESH)
    own = pl.multiple_of((x * 2 + zh) * reads, reads)
    for section in range(section_count):
        part = pl.ds(section * bin_tile, bin_tile)
        keep = pattern_ref[0, section].astype(jnp.float32)
        left[pl.ds(own, reads), part] = (weights_ref[:, part].astype(jnp.float32) * keep).astype(left.dtype)
    pl.semaphore_wait(barrier, len(near))

    row_root = (2 * zl + y // 2, lax.rem(y, 2))
    col_root = (2 * lax.rem(x, 2) + zh, x // 2)
    row_place = lax.rem(x - row_root[0] + 4, 4) + 4 * flip(zh, row_root[1])
    col_place = lax.rem(y - col_root[0] + 4, 4) + 4 * flip(zl, col_root[1])
    row_source = [lax.rem(row_root[0] + s % 4, 4) * 2 + flip(row_root[1], s // 4) for s in range(8)]
    col_source = [lax.rem(x + s % 4, 4) * 2 + flip(zh, s // 4) for s in range(8)]
    row_tile = [pl.multiple_of(a * reads, reads) for a in row_source]
    col_tile = [pl.multiple_of((core * 8 + a) * reads, reads) for a in col_source]

    def in_left(s, c):
        return left.at[pl.ds(row_tile[s] + c * piece, piece)]

    def in_right(s, c):
        return right.at[pl.ds(col_tile[s] + c * piece, piece)]

    def copy(src, dst, way, recv_sem):
        return pltpu.make_async_remote_copy(
            src_ref=src, dst_ref=dst, send_sem=send_sems.at[way], recv_sem=recv_sem, device_id=near[way], device_id_type=MESH
        )

    def handle(kind, role, s, c, ways):
        row_sem = row_sems.at[row_source[s], c]
        col_sem = col_sems.at[col_source[s], c]
        if kind == 0:
            src = in_left(s, c)
            if s != role:
                copy(src, src, XP, row_sem).wait_recv()
        else:
            src = in_right(s, c)
            copy(src, src, YP, col_sem).wait_recv()
        for way in ways:
            if way <= ZH:
                copy(src, src, way, row_sem).start()
            elif way <= ZL:
                copy(src, in_right(s, c), way, col_sem).start()
            else:
                copy(src, in_right(s, c), way, core_sem).start()
        if kind == 0 and role == 0:
            pltpu.make_async_copy(src, in_right(s, c), local_sem).start()

    sent = {}
    for slot in SLOTS:
        for kind, role, entries in slot:
            for entry in entries:
                for way in entry[2:]:
                    at = (0 if way <= ZH else 1, role, way)
                    sent[at] = sent.get(at, 0) + 1

            @pl.when((row_place if kind == 0 else col_place) == role)
            def _(kind=kind, role=role, entries=entries):
                for entry in entries:
                    handle(kind, role, entry[0], entry[1], entry[2:])

    def held(count):
        return right.at[pl.ds(0, count * piece)]

    for (kind, role, way), count in sorted(sent.items()):
        if way == CORE:
            continue

        @pl.when((row_place if kind == 0 else col_place) == role)
        def _(way=way, count=count):
            copy(held(count), held(count), way, core_sem).wait_send()

    every = held(8 * CHUNKS)

    @pl.when(col_place == 0)
    def _():
        pltpu.make_async_copy(every, every, local_sem).wait()

    copy(every, every, CORE, core_sem).wait()


def gather(tile_pattern, weights):
    reads, bins = weights.shape
    return pl.pallas_call(
        gather_kernel,
        out_shape=(pltpu.VMEM((8 * reads, bins), weights.dtype), pltpu.VMEM((16 * reads, bins), weights.dtype)),
        in_specs=[pl.BlockSpec(memory_space=pltpu.SMEM), pl.BlockSpec(memory_space=pltpu.VMEM)],
        out_specs=(pl.BlockSpec(memory_space=pltpu.VMEM), pl.BlockSpec(memory_space=pltpu.VMEM)),
        scratch_shapes=[
            pltpu.SemaphoreType.DMA((7,)),
            pltpu.SemaphoreType.DMA((8, CHUNKS)),
            pltpu.SemaphoreType.DMA((8, CHUNKS)),
            pltpu.SemaphoreType.DMA,
            pltpu.SemaphoreType.DMA,
        ],
        compiler_params=pltpu.CompilerParams(collective_id=0, has_side_effects=True, vmem_limit_bytes=8 << 20),
        name="gather",
    )(tile_pattern, weights)


def product_kernel(scale, left, right, out, left_full, right_full, stage, sems):
    bin_tile = left.shape[1] // left_full.shape[1]
    tile = stage.shape[1]
    rows, cols = left.shape[0] // tile, right.shape[0] // tile
    sections = left_full.shape[1]

    def look(array, full, count):
        @pl.loop(0, count)
        def _(i):
            at = pl.ds(pl.multiple_of(i * tile, tile), tile)
            for s in range(sections):
                top = jnp.max(jnp.abs(array[at, pl.ds(s * bin_tile, bin_tile)]).astype(jnp.float32))
                full[i, s] = (top > 0.0).astype(jnp.int32)

    look(left, left_full, rows)
    look(right, right_full, cols)
    first_row = lax.axis_index("row") * rows
    first_col = lax.axis_index("col") * cols

    def write(i, slot):
        return pltpu.make_async_copy(stage.at[slot], out.at[pl.ds(pl.multiple_of(i * tile, tile), tile)], sems.at[slot])

    @pl.loop(0, rows)
    def _(i):
        slot = lax.rem(i, 2)

        @pl.when(i >= 2)
        def _():
            write(i - 2, slot).wait()

        lhs = pl.ds(pl.multiple_of(i * tile, tile), tile)

        @pl.loop(0, cols)
        def _(j):
            at = pl.ds(pl.multiple_of(j * tile, tile), tile)
            case = left_full[i, 0] * right_full[j, 0] + 2 * left_full[i, 1] * right_full[j, 1]

            def put(part):
                acc = lax.dot_general(left[lhs, part], right[at, part], (((1,), (1,)), ((), ())), preferred_element_type=jnp.float32)
                stage[slot, :, at] = (acc * scale).astype(stage.dtype)

            @pl.when(case == 0)
            def _():
                stage[slot, :, at] = jnp.zeros((tile, tile), stage.dtype)

            @pl.when(case == 1)
            def _():
                put(pl.ds(0, bin_tile))

            @pl.when(case == 2)
            def _():
                put(pl.ds(bin_tile, bin_tile))

            @pl.when(case == 3)
            def _():
                put(pl.ds(0, 2 * bin_tile))

            @pl.when(first_row + i == first_col + j)
            def _():
                shape = (tile, tile)
                same = lax.broadcasted_iota(jnp.int32, shape, 0) == lax.broadcasted_iota(jnp.int32, shape, 1)
                block = stage[slot, :, at].astype(jnp.float32)
                stage[slot, :, at] = jnp.where(same, 0.0, block).astype(stage.dtype)

        write(i, slot).start()

    write(rows - 2, (rows - 2) % 2).wait()
    write(rows - 1, (rows - 1) % 2).wait()


def product(left, right, reads, section_count):
    rows, cols, bins = left.shape[0], right.shape[0], left.shape[1]

    def kernel(*refs):
        product_kernel(1.0 / math.sqrt(bins), *refs)

    return pl.pallas_call(
        kernel,
        out_shape=jax.ShapeDtypeStruct((rows, cols), left.dtype),
        in_specs=[pl.BlockSpec(memory_space=pltpu.VMEM)] * 2,
        out_specs=pl.BlockSpec(memory_space=pl.ANY),
        scratch_shapes=[
            pltpu.SMEM((rows // reads, section_count), jnp.int32),
            pltpu.SMEM((cols // reads, section_count), jnp.int32),
            pltpu.VMEM((2, reads, cols), left.dtype),
            pltpu.SemaphoreType.DMA((2,)),
        ],
        compiler_params=pltpu.CompilerParams(vmem_limit_bytes=16 << 20),
        name="product",
    )(left, right)


def shards(weights, tile_pattern):
    left, right = gather(tile_pattern, weights)
    return product(left, right, weights.shape[0], tile_pattern.shape[1])


def solution(mesh):
    return jax.shard_map(
        shards,
        mesh=mesh,
        in_specs=(P(("row", "col"), None), P(("row", "col"), None)),
        out_specs=P("row", "col"),
        check_vma=False,
    )
```

time: 329 us -> 111 us (0.34)
  the two profiles are of different devices: /device:TPU:7 before, /device:TPU:31 now
where the time goes in v1:
time: 111 us
  Pallas kernels  109 us (98%)
  local copies, waits for them, and re-layouts  1.7 us (2%)
    pallas_call x1, Pallas kernels, gather(): pl.pallas_call(gather_kernel, out_shape=(pltpu.VMEM((8 * reads, bins), we...  69.6 us
    pallas_call x1, Pallas kernels, product(): pl.pallas_call(kernel, out_shape=jax.ShapeDtypeStruct((rows, cols), left....  39.3 us

profile of v1, /device:TPU:31, one launch (start us, length us, event | category | flops | bytes accessed | tf_op | source)
XLA Modules:
  0.0 110.6 jit_solution(16432022187211724649)
XLA Ops:
  0.0 0.0 copy-start
  0.0 1.0 copy-done
  1.0 0.0 copy-start.1
  1.0 0.7 copy-done.1
  1.7 69.6 %gather.1 = (bf16[2048,1024]{1,0:T(8,128)(2,1)S(1)}, bf16[4096,1024]{1,0:T(8,128)(2,1)S(1)}) custom-call(s32[1,2]{1,0:T(1,128)S(1)} %copy-done.1, bf16[256,1024]{1,0:T(8,128)(2,1)S(1)} %copy-done), custom_call_target="tpu_custom_call" | custom-call | tf_op jit(solution)/shard_map/gather/pallas_call | solution.py:519
  71.3 39.3 %product.1 = bf16[2048,4096]{1,0:T(8,128)(2,1)} custom-call(bf16[2048,1024]{1,0:T(8,128)(2,1)S(1)} %get-tuple-element.7.refs_0_, bf16[4096,1024]{1,0:T(8,128)(2,1)S(1)} %get-tuple-element.8.refs_1_), custom_call_target="tpu_custom_call" | custom-call | tf_op jit(solution)/shard_map/product/pallas_call | solution.py:612
Async XLA Ops:
  0.0 1.0 copy-start
  1.0 0.7 copy-start.1

commit v2 on v0

v2 whole, which is shorter than its diff:
```python
import math

import jax
import jax.numpy as jnp
from jax import lax
from jax.experimental import pallas as pl
from jax.experimental.pallas import tpu as pltpu
from jax.sharding import PartitionSpec as P

MESH = pl.DeviceIdType.MESH
CHUNKS = 4
SLOTS = (
    (
        (0,0,((0,0,0,1,4,6),(0,1,0,5,6),(0,2,0,3,6),(0,3,0,2,4,6))),
        (0,1,((1,0,0,1,2),(1,1,0,1),(1,2,1,2),(1,3,1))),
        (0,2,((2,0,0),(2,1,1),(2,2,0,2),(2,3,1))),
        (0,3,((3,0,0,1),(3,1,0,2),(3,2,0,1),(3,3,0,1))),
        (0,4,((4,0,0),(4,1,0,2),(4,2,0,2),(4,3,0,1,2))),
        (0,5,((5,0,0,1,2),(5,1,0,1),(5,2,0,1),(5,3,0,1,2))),
        (0,6,((6,0,0),(6,1,0,2),(6,2,1),(6,3,0,1))),
        (0,7,((7,0,0),(7,1,0,1,2),(7,2,0),(7,3,0,1,2))),
    ),
    (),
    (),
    (),
    (),
    (),
    (),
    (
        (0,0,((4,1,0,4,6),(3,0,3,6),(1,0,5,6))),
        (0,1,((5,0,0,1),(0,0))),
        (0,2,((1,0,0),(3,0,1))),
        (0,3,((2,0,0,2),(0,0,1,2))),
        (0,4,((7,0,0,2),(5,0))),
        (0,5,((1,0,1),(4,0,0))),
        (0,6,((5,0,0),)),
        (0,7,((6,0,0,2),)),
    ),
    (
        (0,1,((2,1,1,2),)),
        (0,5,((6,2,2),)),
        (0,6,((7,1),)),
        (1,3,((0,0,4,6),)),
        (1,4,((0,1,3,4,6),)),
    ),
    (
        (0,3,((7,1,0,1),)),
        (0,7,((4,3,1),(3,1,0,1))),
        (1,1,((0,2,3,5,6),)),
    ),
    (
        (0,6,((2,2,0,1),)),
    ),
    (
        (0,0,((4,2,0,5,6),)),
        (0,2,((6,1,0),)),
    ),
    (
        (0,0,((3,1,0,3,6),(1,1,4,6))),
        (0,1,((0,1,0),(2,3,1,2),(5,3,0,1))),
        (0,2,((1,1,0),(3,2,1))),
        (0,3,((2,2,0),)),
        (0,4,((7,1,0),(5,1,2))),
        (0,5,((4,1,0),(1,2,1))),
        (0,6,((5,1,0),(7,3,1))),
        (0,7,((6,1,0),)),
        (1,3,((0,3,4,5,6),)),
    ),
    (
        (0,5,((6,3,1),)),
    ),
    (
        (0,0,((4,3,0,1,3,6),)),
        (0,4,((0,3,0),)),
    ),
    (
        (0,3,((7,3,1),)),
        (0,7,((2,0,1,0),)),
        (1,1,((3,0,3,6),)),
        (1,2,((0,0,4,5,6),)),
    ),
    (
        (0,0,((7,0,1,0,4,6),(3,2,5,6),(1,2,1,5,6))),
        (0,1,((0,2,0),)),
        (0,2,((5,0),(3,3,1,2))),
        (0,3,((1,0),)),
        (0,4,((7,2,0,2),(5,2,2))),
        (0,5,((4,2,0),)),
        (0,6,((5,2,0),)),
        (0,7,((6,3,2),)),
        (1,5,((0,1,6),)),
        (1,7,((0,1,4,6),)),
    ),
    (
        (0,1,((3,0,2),)),
        (0,3,((6,0,0),)),
        (0,5,((2,2),)),
        (0,6,((4,3),)),
        (0,7,((0,0,0),)),
        (1,2,((0,2,6),)),
        (1,3,((4,1,4,5,6),)),
        (1,4,((1,0,3,4,6),)),
    ),
    (),
    (),
    (
        (0,1,((6,2,0,1),)),
        (0,5,((2,1,1),)),
        (1,1,((3,1,3,6),)),
        (1,2,((0,3,4,6),)),
    ),
    (
        (0,0,((5,1,1,5,6),(3,3,4,6),(1,3,1,3,6))),
        (0,1,((0,3,0),(3,2,2))),
        (0,2,((0,1,0,2),(0,0))),
        (0,3,((6,1,0),(4,3,1))),
        (0,4,((7,3),(5,3,1))),
        (0,5,((4,3),)),
        (0,6,((5,3),(3,1))),
        (0,7,((5,0),)),
        (1,3,((1,1,4,5,6),)),
        (1,5,((0,2,3,6),)),
    ),
    (
        (0,5,((7,3),)),
        (1,4,((4,2,3,4,6),)),
    ),
    (
        (1,1,((0,0,6),)),
        (1,2,((3,0,3,5,6),)),
        (1,7,((0,3,3,4,6),)),
    ),
    (
        (0,5,((2,3,0,1),)),
        (1,1,((4,3,3,5,6),)),
        (1,2,((4,1,4,6),)),
        (1,6,((0,1,5,6),(0,0,4,3,6))),
    ),
    (
        (0,0,((7,2,1,0,3,6),(2,0,0,3,6),(5,0,1,4,6))),
        (0,1,((4,1),)),
        (0,2,((5,3),(7,1,1))),
        (0,3,((1,1,2),)),
        (0,4,((6,0,0),(1,0,1))),
        (0,5,((7,0,0),)),
        (0,6,((4,0,0,2),)),
        (0,7,((2,2,0),)),
        (1,5,((1,0,5,3,6),)),
        (1,7,((1,0,5,6),)),
    ),
    (
        (0,1,((3,3),)),
        (0,3,((7,0,1),)),
        (0,6,((2,0),)),
        (1,3,((7,0,4,6),)),
        (1,4,((3,2,3,4,6),)),
    ),
    (
        (0,0,((5,2,0,3,6),)),
        (1,2,((3,1,3,5,6),)),
    ),
    (
        (1,1,((0,3,6),)),
    ),
    (
        (0,3,((6,3,1,0),)),
        (0,6,((3,3,0,1),)),
        (0,7,((5,3),)),
        (1,1,((1,3,3,6),)),
        (1,2,((1,1,4,6),)),
        (1,5,((4,2,5,6),)),
        (1,6,((0,2,3,6),)),
    ),
    (
        (0,0,((7,1,4,6),(2,1,1,4,6))),
        (0,1,((4,2,0),)),
        (0,2,((0,2,0,2),(7,3,1))),
        (0,3,((0,1),(1,2,1))),
        (0,4,((3,1,0),(1,2,1))),
        (0,5,((7,1),)),
        (0,6,((4,1,0),)),
        (0,7,((5,1),)),
        (1,3,((3,3,4,5,6),(3,0,6))),
        (1,4,((0,3,3,6),)),
        (1,6,((0,3,6),)),
        (1,7,((4,2,5,4,6),)),
    ),
    (
        (1,4,((1,2,3,4,6),)),
    ),
    (
        (0,5,((3,0,1,0),)),
        (1,1,((4,1,6),)),
        (1,2,((0,1,4,3,6),(4,3,3,6))),
        (1,5,((0,0,4,6),)),
        (1,7,((4,1,3,4,6),(0,0,6))),
    ),
    (
        (0,1,((7,1),)),
        (0,7,((1,0,1),)),
        (1,1,((1,0,3,6),)),
        (1,2,((7,0,4,5,6),)),
        (1,3,((1,0,6),)),
    ),
    (
        (0,0,((2,2,0,5,6),(2,3,1,3,5,6))),
        (0,1,((3,1,0),)),
        (0,2,((6,2),(4,3))),
        (0,4,((6,1,0),(6,3))),
        (0,5,((0,3),)),
        (0,6,((0,1,1,0),(4,2,0))),
        (0,7,((5,2),)),
        (1,5,((3,2,5,6),)),
        (1,6,((3,0,4,3,6),(1,0,6))),
        (1,7,((3,2,5,4,6),)),
    ),
    (
        (1,3,((5,0,4,6),(3,1,6))),
        (1,4,((5,1,3,4,6),)),
        (1,5,((4,3,4,3,6),)),
    ),
    (
        (0,5,((3,2,1,0),)),
        (0,7,((1,1,1,0),)),
        (1,1,((2,0,3,5,6),(7,2,5,6))),
    ),
    (
        (0,3,((1,3,1,2),(5,1,1))),
        (0,5,((3,3,1),)),
        (1,1,((1,1,6),)),
        (1,2,((1,3,3,5,6),)),
    ),
    (
        (0,1,((7,3,1),)),
        (0,2,((4,0,1,0),)),
        (0,3,((0,2),)),
        (0,7,((1,2,1),)),
        (1,2,((3,3,4,5,6),)),
        (1,6,((4,2,5,6),)),
        (1,7,((1,1,3,4,6),)),
    ),
    (
        (0,0,((6,0,0,5,6),(5,3,1,4,6))),
        (0,1,((4,3),)),
        (0,2,((0,3,0),(7,0))),
        (0,4,((2,0,0),(2,1,1))),
        (0,5,((7,2,0),)),
        (0,7,((4,0),)),
        (1,1,((4,2,6),)),
        (1,3,((4,2,6),(7,1,4,5,6))),
        (1,4,((4,1,6),)),
        (1,6,((3,1,4,3,6),)),
        (1,7,((1,2,5,4,6),(0,2,5,3,6))),
    ),
    (
        (0,6,((0,2,1,0),)),
        (1,6,((4,1,4,6),)),
    ),
    (
        (0,6,((2,3,0),(7,0),(1,0))),
        (1,1,((0,1,6),)),
        (1,2,((1,0,6),)),
        (1,3,((0,1,6),)),
        (1,4,((0,0,6),)),
        (1,5,((0,3,6),(1,2,5,6))),
    ),
    (
        (1,2,((5,0,4,5,6),)),
        (1,4,((2,2,3,4,6),)),
        (1,5,((3,0,6),)),
        (1,6,((4,3,6),)),
        (1,7,((3,0,3,6),)),
    ),
    (
        (0,0,((6,1,0,4,5,6),(6,2,2,1,3,6))),
        (0,1,((7,0),)),
        (0,2,((4,2,0),(6,3,1))),
        (0,4,((0,0,0),(2,3))),
        (0,5,((0,1),(6,0))),
        (0,7,((3,3),)),
        (1,1,((5,2,3,5,6),(3,2,6))),
        (1,3,((4,3,6),(3,2,4,6))),
        (1,4,((4,3,4,6),)),
        (1,7,((5,1,6),)),
    ),
    (
        (1,3,((2,1,4,5,6),)),
        (1,5,((2,0,4,3,6),(7,2,4,3,6))),
        (1,6,((7,0,3,6),)),
    ),
    (
        (0,6,((1,1),)),
        (1,7,((3,3,6),)),
    ),
    (
        (0,1,((4,0,1),)),
        (0,3,((4,0),(5,0),(7,2,1))),
        (1,1,((7,0,5,6),)),
        (1,2,((2,0,3,6),(4,2,6))),
    ),
    (
        (0,7,((2,1,1),)),
        (1,1,((2,3,3,6),)),
        (1,2,((7,1,4,6),)),
        (1,4,((2,3,3,6),)),
        (1,5,((5,1,3,6),)),
        (1,6,((3,2,6),)),
    ),
    (
        (0,0,((6,3,3,5,6),(7,3,3,4,5,6))),
        (0,2,((3,1),(1,2))),
        (0,4,((2,2),(3,0,1))),
        (0,5,((3,1),(0,2))),
        (0,6,((3,0),)),
        (0,7,((4,1,2),(1,3,1,0))),
        (1,3,((5,3,4,5,6),)),
        (1,4,((1,1,6),(0,2,6))),
        (1,5,((3,1,4,6),)),
        (1,7,((3,1,6),)),
    ),
    (
        (1,1,((1,2,6),)),
        (1,3,((1,3,6),)),
        (1,5,((4,1,6),)),
        (1,6,((1,3,4,3,6),)),
    ),
    (
        (0,1,((2,0),(7,2))),
        (0,6,((1,2),)),
        (1,1,((3,3,6),)),
        (1,2,((5,2,3,6),)),
        (1,3,((0,2,6),)),
        (1,7,((7,1,3,4,6),(2,2,5,6))),
    ),
    (
        (0,1,((6,3),)),
        (0,3,((0,3,2),)),
        (1,4,((6,0,3,4,6),)),
        (1,5,((5,2,4,6),)),
        (1,6,((1,2,5,6),)),
    ),
    (
        (0,4,((1,1,0),)),
        (0,5,((6,1),)),
        (1,1,((6,2,3,5,6),)),
        (1,3,((1,2,6),)),
        (1,4,((3,0,6),)),
        (1,5,((2,2,5,3,6),)),
        (1,6,((2,0,3,6),(7,2,5,6))),
        (1,7,((7,0,3,6),)),
    ),
    (
        (0,3,((2,1),)),
        (0,4,((3,2,1),)),
        (0,6,((3,2),)),
        (1,2,((2,1,4,6),)),
        (1,3,((6,1,4,6),(2,0,6))),
        (1,4,((2,0,6),(7,2,4,6))),
        (1,6,((1,1,4,6),(3,3,4,6))),
        (1,7,((4,3,6),)),
    ),
    (
        (0,0,((4,0,3,4,5,6),)),
        (0,7,((0,1,0),(4,2))),
        (1,7,((2,1,3,4,6),)),
    ),
    (
        (0,2,((1,3),(5,1,1))),
        (0,3,((4,2),)),
        (1,1,((5,0,5,6),)),
        (1,2,((2,3,3,5,6),(3,2,6))),
    ),
    (
        (0,4,((3,3),)),
        (0,6,((7,2),(2,1))),
        (0,7,((3,0),)),
        (1,4,((6,1,3,4,6),)),
        (1,5,((7,0,6),(2,3,6))),
    ),
    (
        (0,1,((5,2,0),)),
        (0,3,((2,3),)),
        (0,5,((2,0),)),
        (1,1,((6,3,3,6),)),
        (1,3,((7,3,6),)),
        (1,4,((3,1,6),)),
        (1,5,((1,3,6),)),
    ),
    (
        (0,4,((1,3,0),)),
        (1,3,((5,2,5,6),)),
        (1,6,((5,1,5,6),(5,0,3,6))),
        (1,7,((1,3,3,6),)),
    ),
    (
        (0,4,((6,2,1),)),
        (0,6,((1,3),)),
        (1,1,((7,1,6),)),
        (1,3,((2,2,4,6),)),
        (1,6,((7,1,4,6),)),
        (1,7,((5,3,3,4,6),)),
    ),
    (
        (0,3,((4,1,1),)),
        (1,1,((2,2,6),)),
        (1,2,((6,2,3,6),(5,3,4,6))),
        (1,4,((7,1,6),)),
        (1,7,((2,0,6),)),
    ),
    (
        (0,1,((2,2),)),
        (0,2,((7,2),)),
        (0,5,((0,0,0),)),
        (0,7,((0,3,1),)),
        (1,1,((7,3,3,6),)),
        (1,2,((7,2,6),)),
        (1,5,((6,0,5,3,6),(6,2,4,3,6))),
        (1,7,((6,0,5,6),)),
    ),
    (
        (0,1,((5,1),)),
        (0,3,((5,3),)),
        (0,7,((3,2),(0,2,0))),
        (1,2,((1,2,6),)),
        (1,3,((4,0,5,6),(2,3,6))),
        (1,4,((5,2,6),(6,3,3,4,6))),
        (1,5,((3,3,4,6),)),
        (1,7,((7,2,5,6),)),
    ),
    (
        (0,4,((0,1),)),
        (1,4,((7,0,6),)),
        (1,5,((1,1,6),)),
        (1,6,((2,2,6),)),
    ),
    (
        (0,2,((5,2,0),)),
        (1,1,((2,1,5,6),)),
        (1,2,((6,3,3,6),)),
        (1,6,((2,1,6),)),
    ),
    (
        (0,7,((2,3),)),
        (1,2,((6,1,5,6),)),
        (1,5,((6,1,5,6),)),
        (1,6,((2,3,3,6),)),
    ),
    (
        (0,1,((6,0,0),)),
        (0,3,((6,2),)),
        (0,5,((1,1),)),
        (1,1,((4,0,3,5,6),)),
        (1,5,((5,0,4,6),)),
        (1,7,((5,2,4,6),(6,1,6),(5,0,6))),
    ),
    (
        (1,3,((6,2,5,6),)),
        (1,4,((7,3,3,4,6),)),
    ),
    (
        (0,2,((4,1),)),
        (0,7,((6,2),)),
        (1,1,((5,3,6),)),
        (1,2,((5,1,4,3,6),)),
        (1,3,((6,0,6),)),
        (1,4,((2,1,6),)),
    ),
    (
        (0,6,((0,0),(0,3))),
        (1,1,((6,0,3,6),)),
        (1,2,((7,3,5,6),(2,2,6))),
        (1,3,((7,2,6),)),
        (1,6,((5,3,4,6),)),
    ),
    (
        (0,1,((6,1),)),
        (0,5,((1,3),)),
        (1,5,((7,1,6),(6,3,3,6))),
        (1,6,((6,0,6),(6,2,6))),
        (1,7,((4,0,4,6),)),
    ),
    (
        (0,4,((0,2),)),
        (1,4,((3,3,6),(4,0,6))),
    ),
    (
        (0,3,((5,2),)),
        (1,3,((6,3,6),)),
        (1,4,((6,2,6),(1,3,6))),
        (1,5,((2,1,6),)),
        (1,7,((6,3,6),)),
    ),
    (
        (0,2,((6,0),)),
        (1,1,((6,1,6),)),
        (1,2,((4,0,6),)),
        (1,6,((6,1,6),)),
        (1,7,((2,3,6),)),
    ),
    (
        (1,5,((7,3,6),)),
        (1,6,((5,2,6),)),
    ),
    (
        (1,7,((6,2,6),)),
    ),
    (
        (1,1,((5,1,6),)),
        (1,4,((5,3,6),(5,0,6))),
        (1,5,((4,0,6),(5,3,6))),
        (1,7,((7,3,6),)),
    ),
    (
        (1,3,((5,1,6),)),
        (1,6,((7,3,6),)),
    ),
    (
        (1,2,((6,0,6),)),
        (1,6,((6,3,6),(4,0,6))),
    ),
    (),
    (),
    (),
    (),
    (),
    (),
    (),
    (),
)
ROW_ORDER = ((0,3,1,2,5,6,7,4),(1,0,3,4,7,2,5,6),(2,0,3,1,7,5,4,6),(3,1,7,0,2,4,6,5),(4,7,5,2,3,1,6,0),(5,4,7,3,6,2,0,1),(6,5,4,3,7,2,1,0),(7,5,1,4,3,0,2,6))
COL_ORDER = ((0,3,1,2,5,6,7,4),(0,1,3,7,2,4,6,5),(0,3,1,5,7,2,4,6),(3,0,1,4,2,7,6,5),(0,7,2,3,4,6,1,5),(0,3,1,6,2,7,4,5),(0,1,3,2,5,7,6,4),(0,3,1,5,4,2,6,7))
READY = (51, 69, 70, 73, 76, 80, 80, 81)
STEPS = ((0,0),(1,0),(2,0),(3,0),(4,0),(5,0),(6,0),(0,1),(1,1),(2,1),(3,1),(4,1),(5,1),(6,1),(0,2),(1,2),(2,2),(3,2),(4,2),(5,2),(6,2),(7,0),(7,1),(7,2))
FIRST_STEP = 63
XP, XM, ZH, YP, YM, ZL, CORE = range(7)


def place():
    row, col = lax.axis_index("row"), lax.axis_index("col")
    return col // 2, lax.rem(col, 2), lax.rem(row // 2, 4), row // 8, lax.rem(row, 2)


def device(x, zh, y, zl, core):
    return (zl * 8 + y * 2 + core, x * 2 + zh)


def neighbours(x, zh, y, zl, core):
    def turn(a, by):
        return lax.rem(a + by, 4)

    return {
        XP: device(turn(x, 1), zh, y, zl, core),
        XM: device(turn(x, 3), zh, y, zl, core),
        ZH: device(x, 1 - zh, y, zl, core),
        YP: device(x, zh, turn(y, 1), zl, core),
        YM: device(x, zh, turn(y, 3), zl, core),
        ZL: device(x, zh, y, 1 - zl, core),
        CORE: device(x, zh, y, zl, 1 - core),
    }


def flip(a, b):
    return a + b - 2 * a * b


def pick(values, at):
    out = jnp.int32(values[0])
    for n, value in enumerate(values[1:], 1):
        out = jnp.where(at == n, jnp.int32(value), out)
    return out


def packed(entries, bits):
    out = 0
    for n, entry in enumerate(entries):
        out += entry << (bits * n)
    return out


def digit(code, at, bits):
    return lax.rem(lax.shift_right_logical(code, bits * at), 1 << bits)


class Place:
    def __init__(self):
        self.coordinates = x, zh, y, zl, core = place()
        self.core = core
        self.row_root = (2 * zl + y // 2, lax.rem(y, 2))
        self.col_root = (2 * lax.rem(x, 2) + zh, x // 2)
        self.row_place = lax.rem(x - self.row_root[0] + 4, 4) + 4 * flip(zh, self.row_root[1])
        self.col_place = lax.rem(y - self.col_root[0] + 4, 4) + 4 * flip(zl, self.col_root[1])
        self.row_code = pick([packed(order, 3) for order in ROW_ORDER], self.row_place)
        self.col_code = pick([packed(order, 3) for order in COL_ORDER], self.col_place)

    def row_shard(self, source):
        return lax.rem(self.row_root[0] + lax.rem(source, 4), 4) * 2 + flip(self.row_root[1], source // 4)

    def col_shard(self, source):
        return lax.rem(self.coordinates[0] + lax.rem(source, 4), 4) * 2 + flip(self.coordinates[1], source // 4)

    def row_ranked(self, rank):
        return self.row_shard(digit(self.row_code, rank, 3))

    def col_ranked(self, rank):
        return self.col_shard(digit(self.col_code, rank, 3))


def dot(lhs, rhs):
    return lax.dot_general(lhs, rhs, (((1,), (1,)), ((), ())), preferred_element_type=jnp.float32)


def clear_diagonal(block):
    same = lax.broadcasted_iota(jnp.int32, block.shape, 0) == lax.broadcasted_iota(jnp.int32, block.shape, 1)
    return jnp.where(same, 0.0, block.astype(jnp.float32)).astype(block.dtype)


def gather_kernel(
    scale, pattern_ref, weights_ref, left, right, blocks, send_sems, row_sems, col_sems, core_sems, local_sems
):
    reads, bins = weights_ref.shape
    section_count = pattern_ref.shape[1]
    bin_tile = bins // section_count
    piece = reads // CHUNKS
    x, zh, y, zl, core = place()
    near = neighbours(x, zh, y, zl, core)
    barrier = pltpu.get_barrier_semaphore()
    for target in near.values():
        pl.semaphore_signal(barrier, inc=1, device_id=target, device_id_type=MESH)
    own = pl.multiple_of((x * 2 + zh) * reads, reads)
    for section in range(section_count):
        part = pl.ds(section * bin_tile, bin_tile)
        keep = pattern_ref[0, section].astype(jnp.float32)
        left[pl.ds(own, reads), part] = (weights_ref[:, part].astype(jnp.float32) * keep).astype(left.dtype)
    pl.semaphore_wait(barrier, len(near))

    here = Place()
    row_place, col_place = here.row_place, here.col_place
    row_source = [here.row_shard(s) for s in range(8)]
    col_source = [here.col_shard(s) for s in range(8)]
    row_tile = [pl.multiple_of(a * reads, reads) for a in row_source]
    col_tile = [pl.multiple_of((core * 8 + a) * reads, reads) for a in col_source]

    def in_left(s, c):
        return left.at[pl.ds(row_tile[s] + c * piece, piece)]

    def in_right(s, c):
        return right.at[pl.ds(col_tile[s] + c * piece, piece)]

    def copy(src, dst, way, recv_sem):
        return pltpu.make_async_remote_copy(
            src_ref=src, dst_ref=dst, send_sem=send_sems.at[way], recv_sem=recv_sem, device_id=near[way], device_id_type=MESH
        )

    def handle(kind, role, s, c, ways):
        row_sem = row_sems.at[row_source[s], c]
        col_sem = col_sems.at[col_source[s], c]
        if kind == 0:
            src = in_left(s, c)
            if s != role:
                copy(src, src, XP, row_sem).wait_recv()
        else:
            src = in_right(s, c)
            copy(src, src, YP, col_sem).wait_recv()
        for way in ways:
            if way <= ZH:
                copy(src, src, way, row_sem).start()
            elif way <= ZL:
                copy(src, in_right(s, c), way, col_sem).start()
            else:
                copy(src, in_right(s, c), way, core_sems.at[col_source[s]]).start()
        if kind == 0 and role == 0:
            pltpu.make_async_copy(src, in_right(s, c), local_sems.at[col_source[s]]).start()

    def shard_ready(rank):
        shard = here.col_ranked(rank)
        block = right.at[pl.ds(pl.multiple_of(shard * reads, reads), reads)]
        copy(block, block, CORE, core_sems.at[shard]).wait_recv()

        @pl.when(col_place == 0)
        def _():
            pltpu.make_async_copy(block, block, local_sems.at[shard]).wait()

    first_row = lax.axis_index("row") * 8
    first_col = lax.axis_index("col") * 16

    def multiply(step):
        per = 5
        codes = [packed([a * 8 + b for a, b in STEPS[n : n + per]], 6) for n in range(0, len(STEPS), per)]
        pair = digit(pick(codes, step // per), lax.rem(step, per), 6)
        i, shard = here.row_ranked(pair // 8), here.col_ranked(lax.rem(pair, 8))
        rows = pl.ds(pl.multiple_of(i * reads, reads), reads)
        for half in range(2):
            j = half * 8 + shard
            tile = pl.ds(pl.multiple_of(j * reads, reads), reads)
            blocks[j, rows, :] = (dot(left[rows, :], right[tile, :]) * scale).astype(blocks.dtype)
        for half in range(2):
            j = half * 8 + shard

            @pl.when(first_row + i == first_col + j)
            def _(j=j):
                blocks[j, rows, :] = clear_diagonal(blocks[j, rows, :])

    sent = {}

    def run_slot(slot):
        for kind, role, entries in SLOTS[slot]:
            for entry in entries:
                for way in entry[2:]:
                    at = (0 if way <= ZH else 1, role, way)
                    sent[at] = sent.get(at, 0) + 1

            @pl.when((row_place if kind == 0 else col_place) == role)
            def _(kind=kind, role=role, entries=entries):
                for entry in entries:
                    handle(kind, role, entry[0], entry[1], entry[2:])

        for rank, at in enumerate(READY):
            if at == slot:
                shard_ready(rank)

    def dispatch(slot, low, high):
        if high - low == 1:
            run_slot(low)
            return
        middle = (low + high) // 2

        @pl.when(slot < middle)
        def _():
            dispatch(slot, low, middle)

        @pl.when(slot >= middle)
        def _():
            dispatch(slot, middle, high)

    @pl.loop(0, len(SLOTS))
    def _(slot):
        dispatch(slot, 0, len(SLOTS))

        @pl.when(jnp.logical_and(slot >= FIRST_STEP, slot < FIRST_STEP + len(STEPS)))
        def _():
            multiply(slot - FIRST_STEP)

    def held(count):
        return right.at[pl.ds(0, count * piece)]

    for (kind, role, way), count in sorted(sent.items()):

        @pl.when((row_place if kind == 0 else col_place) == role)
        def _(way=way, count=count):
            copy(held(count), held(count), way, core_sems.at[0]).wait_send()


def gather(tile_pattern, weights):
    reads, bins = weights.shape

    def kernel(*refs):
        gather_kernel(1.0 / math.sqrt(bins), *refs)

    return pl.pallas_call(
        kernel,
        out_shape=(
            pltpu.VMEM((8 * reads, bins), weights.dtype),
            pltpu.VMEM((16 * reads, bins), weights.dtype),
            pltpu.VMEM((16, 8 * reads, reads), weights.dtype),
        ),
        in_specs=[pl.BlockSpec(memory_space=pltpu.SMEM), pl.BlockSpec(memory_space=pltpu.VMEM)],
        out_specs=(pl.BlockSpec(memory_space=pltpu.VMEM),) * 3,
        scratch_shapes=[
            pltpu.SemaphoreType.DMA((7,)),
            pltpu.SemaphoreType.DMA((8, CHUNKS)),
            pltpu.SemaphoreType.DMA((8, CHUNKS)),
            pltpu.SemaphoreType.DMA((8,)),
            pltpu.SemaphoreType.DMA((8,)),
        ],
        compiler_params=pltpu.CompilerParams(collective_id=0, has_side_effects=True, vmem_limit_bytes=8 << 20),
        name="gather",
    )(tile_pattern, weights)


def finish_kernel(scale, done, left, right, blocks, out, stage, sems):
    here = Place()
    tile = blocks.shape[2]
    rows = left.shape[0] // tile
    first_row = lax.axis_index("row") * rows
    first_col = lax.axis_index("col") * 16

    def panel(n):
        return lax.rem(n, 2) * 8 + here.col_ranked(n // 2)

    def write(n, src):
        return pltpu.make_async_copy(src, out.at[:, pl.ds(pl.multiple_of(panel(n) * tile, tile), tile)], sems.at[n])

    for n in range(done):
        write(n, blocks.at[panel(n)]).start()

    @pl.loop(0, 16 - done)
    def _(n):
        j = panel(done + n)
        at = pl.ds(pl.multiple_of(j * tile, tile), tile)
        stage[n] = (dot(left[...], right[at, :]) * scale).astype(stage.dtype)
        i = first_col + j - first_row

        @pl.when(jnp.logical_and(i >= 0, i < rows))
        def _():
            part = pl.ds(pl.multiple_of(i * tile, tile), tile)
            stage[n, part, :] = clear_diagonal(stage[n, part, :])

        write(done + n, stage.at[n]).start()

    for n in range(16):
        write(n, blocks.at[n]).wait()


def finish(left, right, blocks):
    rows, bins = left.shape
    count, _, tile = blocks.shape
    done = 2 * (1 + max(b for _, b in STEPS))

    def kernel(*refs):
        finish_kernel(1.0 / math.sqrt(bins), done, *refs)

    return pl.pallas_call(
        kernel,
        out_shape=jax.ShapeDtypeStruct((rows, count * tile), left.dtype),
        in_specs=[pl.BlockSpec(memory_space=pltpu.VMEM)] * 3,
        out_specs=pl.BlockSpec(memory_space=pl.ANY),
        scratch_shapes=[pltpu.VMEM((max(16 - done, 1), rows, tile), left.dtype), pltpu.SemaphoreType.DMA((count,))],
        compiler_params=pltpu.CompilerParams(vmem_limit_bytes=16 << 20),
        name="finish",
    )(left, right, blocks)


def shards(weights, tile_pattern):
    return finish(*gather(tile_pattern, weights))


def solution(mesh):
    return jax.shard_map(
        shards,
        mesh=mesh,
        in_specs=(P(("row", "col"), None), P(("row", "col"), None)),
        out_specs=P("row", "col"),
        check_vma=False,
    )
```

time: 329 us -> 87.9 us (0.27)
  waiting for transfers between devices: 249 us -> 0 us
  Pallas kernels: 0 us -> 86 us
  matrix products: 22.5 us -> 0 us
  local copies, waits for them, and re-layouts: 22.1 us -> 1.7 us
  other arithmetic: 19 us -> 0 us
  between operations: 13.2 us -> 0.01 us
    psum x1 -> x0, waiting for transfers between devices: 143 us -> none  [from_root(): return lax.psum(kept, axis)]
    all_gather x2 -> x0, waiting for transfers between devices: 106 us -> none  [shards(): left_piece = lax.all_gather(panel_rows, 'col', axis=0, tiled=True)]
    pallas_call x0 -> x2, Pallas kernels: none -> 86 us  [the longest x1 71.7 us: gather(): pl.pallas_call(kernel, out_shape=(pltpu.VMEM((8 * reads, bins), weights.d...]
    dot_general x2 -> x0, matrix products: 22.5 us -> none  [shards(): lax.dot_general(left_side, right_side, (((1,), (1,)), ((), ())), preferre...]
    reshape x1 -> x0, local copies, waits for them, and re-layouts: 21.2 us -> none  [shards(): return jnp.transpose(stacked, (1, 0, 2)).reshape(row_block, col_block)]
    select_n x2 -> x0, other arithmetic: 10.4 us -> none  [from_root(): jnp.where(lax.axis_index(axis) == source, value, 0).astype(value.dtype)]
    another operation x1 -> x0, other arithmetic: 6.82 us -> none  [shards(): stacked = jnp.stack(blocks, axis=0)]
  transfers between devices with their start and end apart: 3 -> 0, of which waited for: 3 -> 0; matrix products, arithmetic and copies ran while one was open for 1% -> 0% of each run, Pallas kernels for 0% -> 0%
where the time goes in v2:
time: 87.9 us; the launch traced here: 87.8 us
  Pallas kernels  86 us (98%)
  local copies, waits for them, and re-layouts  1.7 us (2%)
    pallas_call x1, Pallas kernels, gather(): pl.pallas_call(kernel, out_shape=(pltpu.VMEM((8 * reads, bins), weights.d...  71.7 us
    pallas_call x1, Pallas kernels, finish(): pl.pallas_call(kernel, out_shape=jax.ShapeDtypeStruct((rows, count * tile...  14.3 us

profile of v2, /device:TPU:7, one launch (start us, length us, event | category | flops | bytes accessed | tf_op | source)
XLA Modules:
  0.0 87.8 jit_solution(8125437524724414939)
XLA Ops:
  0.0 0.0 copy-start
  0.0 1.0 %copy-done = bf16[256,1024]{1,0:T(8,128)(2,1)S(1)} copy-done((bf16[256,1024]{1,0:T(8,128)(2,1)S(1)}, bf16[256,1024]{1,0:T(8,128)(2,1)}, u32[]{:S(2)}) %copy-start) | copy-done | bytes 524312
  1.0 0.0 copy-start.1
  1.0 0.7 copy-done.1
  1.7 71.7 %gather.1 = (bf16[2048,1024]{1,0:T(8,128)(2,1)S(1)}, bf16[4096,1024]{1,0:T(8,128)(2,1)S(1)}, bf16[16,2048,256]{2,1,0:T(8,128)(2,1)S(1)}) custom-call(s32[1,2]{1,0:T(1,128)S(1)} %copy-done.1, bf16[256,1024]{1,0:T(8,128)(2,1)S(1)} %copy-done), custom_call_target="tpu_custom_call" | custom-call | tf_op jit(solution)/shard_map/gather/pallas_call | solution.py:759
  73.4 14.3 %finish.1 = bf16[2048,4096]{1,0:T(8,128)(2,1)} custom-call(bf16[2048,1024]{1,0:T(8,128)(2,1)S(1)} %get-tuple-element.8.refs_0_, bf16[4096,1024]{1,0:T(8,128)(2,1)S(1)} %get-tuple-element.9.refs_1_, bf16[16,2048,256]{2,1,0:T(8,128)(2,1)S(1)} %get-tuple-element.10.refs_2_), custom_call_target="tpu_custom_call" | custom-call | tf_op jit(solution)/shard_map/finish/pallas_call | solution.py:822
Async XLA Ops:
  0.0 1.0 %copy-start = (bf16[256,1024]{1,0:T(8,128)(2,1)S(1)}, bf16[256,1024]{1,0:T(8,128)(2,1)}, u32[]{:S(2)}) copy-start(bf16[256,1024]{1,0:T(8,128)(2,1)} %refs_1_.1) | copy-start | bytes 1572868
  1.0 0.7 copy-start.1

commit v3 on v0

v3 whole, which is shorter than its diff:
```python
import math

import jax
import jax.numpy as jnp
from jax import lax
from jax.experimental import pallas as pl
from jax.experimental.pallas import tpu as pltpu
from jax.sharding import PartitionSpec as P

MESH = pl.DeviceIdType.MESH
CHUNKS = 8
UNITS = 2
SLOTS = (
    (
        (0,0,((0,0,1,5),(0,1,0,1,4),(0,2,1,4),(0,3,0,3,6),(0,4,0,1,4),(0,5,0,3),(0,6,1,5),(0,7,0,1,5,6))),
        (0,1,((1,0,0,1),(1,1,0,1,2),(1,2,0,1,2),(1,3,0),(1,4,0,1),(1,5,0,2),(1,6,0,1),(1,7,0,2))),
        (0,2,((2,0,1,2),(2,1,0,2),(2,2,1),(2,3,0,1,2),(2,4,0,2),(2,5,0,1,2),(2,6,1),(2,7,2))),
        (0,3,((3,0,0,2),(3,1,0,1,2),(3,2,2),(3,3,1),(3,4,1),(3,5,0),(3,6,0,2),(3,7,0,1,2))),
        (0,4,((4,0,0,2),(4,1,0,2),(4,2,0,1),(4,3,0,1),(4,4,1,2),(4,5,0,1),(4,6,0,1,2),(4,7,0,1,2))),
        (0,5,((5,0,1,2),(5,1,1),(5,2,0,1),(5,3,0,2),(5,4,0,1),(5,5,2),(5,6,1,2),(5,7,1,2))),
        (0,6,((6,0,0),(6,1,0,2),(6,2,1,2),(6,3,0,2),(6,4,1,2),(6,5,0),(6,6,0,2),(6,7,1,2))),
        (0,7,((7,0,1),(7,1,0,1),(7,2,0,1,2),(7,3,0,1),(7,4,2),(7,5,1),(7,6,1),(7,7,0,1,2))),
    ),
    (),
    (),
    (),
    (),
    (
        (0,0,((3,0,0,4),(1,0,1,3))),
        (0,1,((2,0),(0,1))),
        (0,2,((1,0,2),(3,1,2))),
        (0,3,((0,0,1),(2,1,0))),
        (0,4,((5,0,1),(7,1,0,2))),
        (0,5,((4,0,0,2),)),
        (0,6,((7,0,1,2),)),
        (0,7,((6,0,0),)),
        (1,4,((0,0,3),)),
    ),
    (
        (0,0,((4,0,1,3,5),)),
        (0,1,((5,0,0,1),)),
        (0,5,((6,2,1),)),
        (0,6,((5,2),(2,0,1))),
        (0,7,((4,2,1,2),(3,0,0))),
        (1,1,((0,3,3),)),
        (1,3,((0,1,4),)),
    ),
    (
        (0,0,((3,1,4),(1,1,5))),
        (0,1,((2,2,1,2),)),
        (0,2,((6,1,0),(1,1,0))),
        (0,3,((7,2,1),(0,1,1))),
        (0,4,((5,1,1,2),)),
        (0,5,((1,1,0),(4,1,0))),
        (0,6,((7,1),)),
        (0,7,((6,1,0),)),
        (1,4,((0,6,3,4),)),
    ),
    (
        (0,1,((0,3,0),)),
        (0,2,((3,3,1,2),)),
        (0,3,((2,3,0),)),
        (0,4,((7,2,0),)),
        (0,5,((6,4,1,2),)),
        (0,6,((5,3,0),)),
        (0,7,((4,3,2),)),
        (1,3,((0,2,4,5),)),
    ),
    (
        (0,0,((4,1,1,3),)),
        (0,1,((5,3,0),)),
        (0,2,((6,2,1),)),
        (0,3,((7,4,0,1),)),
        (0,5,((1,2,0),)),
        (0,6,((2,1,1),)),
        (0,7,((3,1),)),
        (1,1,((0,5,3,5),)),
    ),
    (
        (0,0,((3,5,0,5),(1,2,1,5))),
        (0,1,((2,3),(0,4))),
        (0,2,((1,2),(3,4,1,2))),
        (0,3,((0,2,1),(2,4,0))),
        (0,4,((5,2,1),(7,3,0))),
        (0,5,((4,2),(6,7,1))),
        (0,6,((7,2),(5,4))),
        (0,7,((6,3,0),(4,4,1))),
        (1,3,((0,4,4),)),
        (1,4,((0,7,3,4),)),
    ),
    (
        (0,0,((4,4,1,3),)),
        (0,1,((5,5,0),)),
        (0,2,((6,3,1),)),
        (0,3,((7,7,0,1),)),
        (0,5,((1,5,1),)),
        (0,6,((2,3,1),)),
        (0,7,((3,2,0,1),)),
        (1,1,((1,0,3),)),
        (1,2,((0,1,4,5),)),
        (1,5,((0,0,5,3),)),
    ),
    (
        (0,0,((3,6,5),(1,4,1,4))),
        (0,1,((2,5),(0,5,0))),
        (0,2,((1,3,0,2),(3,7,1))),
        (0,3,((0,4,1,2),(2,5,0))),
        (0,4,((5,4,2),(7,7,0))),
        (0,5,((4,3,0,2),(7,0,1))),
        (0,6,((7,3,2),(4,0,0))),
        (0,7,((6,5,0,2),(4,5))),
        (1,2,((0,3,3,5),)),
        (1,3,((3,0,4,5),)),
        (1,4,((4,0,3,4),)),
    ),
    (
        (0,0,((4,6,0,4),)),
        (0,1,((5,6,0,1),)),
        (0,2,((6,4),)),
        (0,5,((1,7,1),)),
        (0,6,((2,4,0),)),
        (0,7,((3,6,0,1),)),
        (1,1,((4,0,3),)),
        (1,5,((0,6),)),
        (1,7,((0,6,5,4),)),
    ),
    (
        (0,0,((3,7,5),(1,6,3))),
        (0,1,((2,6,1,2),(0,7))),
        (0,2,((1,4,2),(0,0,1,2))),
        (0,3,((4,2,0,1),(0,6,1,2),(6,1,0))),
        (0,4,((5,6,1),(6,0,0,2))),
        (0,5,((4,5,0,2),)),
        (0,6,((7,5,2),)),
        (0,7,((6,6,0),)),
        (1,2,((0,2,4),(0,5,3))),
        (1,4,((1,1,3,4),)),
    ),
    (
        (0,0,((4,7,0,1,3),)),
        (0,1,((5,7,0,1),)),
        (0,5,((2,0,1),)),
        (0,6,((1,1,0),(2,5,0))),
        (0,7,((4,6,1,2),(3,7,1))),
        (1,3,((3,1,4,5),)),
    ),
    (
        (0,0,((2,1,0,4),(5,0,1,4))),
        (0,1,((3,3,1,2),)),
        (0,2,((6,6,0),(1,5,0))),
        (0,3,((4,3,1),(0,7,1,2))),
        (0,4,((5,7,1),)),
        (0,5,((2,2,0,1),(4,6))),
        (0,6,((7,6,1,2),)),
        (0,7,((5,3,0),)),
        (1,1,((4,1,3),)),
        (1,2,((0,4,4,5),)),
        (1,5,((0,7,5,3),)),
        (1,7,((0,7),)),
    ),
    (
        (0,1,((3,0,0),)),
        (0,2,((7,2,1),)),
        (0,3,((1,1),)),
        (0,4,((3,0,0),)),
        (0,5,((2,1,1),)),
        (0,6,((4,1,0),)),
        (0,7,((4,7),)),
        (1,1,((0,1),)),
        (1,2,((1,0,3,5),)),
        (1,4,((3,5,3,4),)),
        (1,6,((0,0,3),(0,1,4,3))),
    ),
    (
        (0,0,((7,1,4),)),
        (0,1,((4,0,0),)),
        (0,2,((6,7,0,1),)),
        (0,6,((2,7,0),)),
        (1,1,((4,4,3,5),)),
        (1,2,((3,0,4),)),
        (1,3,((1,4,4,5),(0,3))),
        (1,5,((4,0),)),
        (1,7,((4,0,4),)),
    ),
    (
        (0,0,((2,3,4,5),(2,2,1,3))),
        (0,1,((6,2,1),(3,5,0,2))),
        (0,2,((1,6,0,2),(0,1,2))),
        (0,3,((1,0),(1,3,0))),
        (0,4,((6,2,1),(6,1,0))),
        (0,5,((4,7,0),(2,3,1))),
        (0,6,((7,7),(1,2,0))),
        (0,7,((4,0),(5,0))),
        (1,2,((4,0,3),)),
        (1,4,((1,2,3,4),)),
        (1,6,((0,6,5),)),
    ),
    (
        (0,0,((5,1,0,1,5),)),
        (0,1,((6,4,1),)),
        (0,2,((7,0,0,1),)),
        (0,3,((6,5,1,0),)),
        (0,6,((1,0,1,0),)),
        (0,7,((0,4,0),)),
        (1,1,((0,0,3),(0,2,6),(1,6,3,5))),
        (1,2,((3,1,4),)),
        (1,3,((4,6,4),(0,5))),
        (1,5,((0,5,4,3),(1,1,5))),
        (1,7,((0,2,3,4),(1,1,4))),
    ),
    (
        (0,0,((7,4,0,3),(5,6,1,5))),
        (0,1,((3,4,1),(4,6,0))),
        (0,2,((1,7),(7,4))),
        (0,3,((4,0),(6,6,0))),
        (0,4,((6,4,1),(6,3,0))),
        (0,5,((7,1,2),)),
        (0,6,((4,2),(4,3))),
        (0,7,((2,4,0),(5,1,1))),
        (1,4,((3,6,3,4),)),
        (1,6,((0,3,4,3),)),
    ),
    (
        (0,5,((2,6,0,1),(7,6,1))),
        (0,6,((3,1,1),)),
        (1,1,((0,4),(4,7,3,5))),
        (1,2,((4,1,3,5),)),
        (1,3,((2,1,4),(0,6))),
        (1,6,((0,7,5),)),
        (1,7,((0,0),)),
    ),
    (
        (0,0,((2,4,0,5),(2,6,1,3,4))),
        (0,1,((6,3,1),(4,7))),
        (0,2,((5,0,2),(7,3,0,1),(0,2,1,2))),
        (0,3,((4,1,1),(4,6),(1,5,2))),
        (0,4,((6,7,1),(3,2,2,0))),
        (0,5,((7,2),)),
        (0,6,((4,4,1),)),
        (0,7,((1,1,0),(0,6,0,1))),
        (1,2,((1,4),)),
        (1,3,((1,0),)),
        (1,4,((3,7,3,4),)),
        (1,5,((3,5,5),(0,1))),
        (1,7,((3,5,5,4),)),
    ),
    (
        (0,0,((5,4,0,1,4,5),)),
        (0,1,((4,3,1),)),
        (0,5,((3,3,1),)),
        (0,6,((4,5),(3,3))),
        (0,7,((5,2,2),)),
        (1,2,((4,4,3),)),
        (1,6,((4,0),)),
        (1,7,((3,0,3,4),)),
    ),
    (
        (0,0,((7,7,0,3),(5,7,4))),
        (0,1,((3,7),)),
        (0,2,((0,3,0,2),)),
        (0,3,((1,2),)),
        (0,4,((1,5,2),)),
        (0,5,((7,3),(1,0))),
        (0,6,((3,2,2),)),
        (0,7,((2,5,0),(0,7,1))),
        (1,1,((2,2,5),(3,0))),
        (1,3,((5,0,4),(4,0))),
        (1,5,((1,2,3),)),
        (1,7,((0,1,3),(1,2,5))),
    ),
    (
        (0,1,((2,1),)),
        (0,2,((7,7),)),
        (0,3,((6,7),)),
        (0,4,((6,5,0),)),
        (0,6,((2,2,0),)),
        (0,7,((5,6,1),)),
        (1,2,((0,6,4),(4,6,5))),
        (1,4,((2,3,4),(0,2,3),(0,5))),
        (1,6,((0,5,3),(0,2,6))),
    ),
    (
        (0,1,((4,5,1,0),)),
        (0,2,((7,5,0,1),)),
        (0,6,((3,4,1),)),
        (1,1,((3,1),(7,4,3,5))),
        (1,2,((0,0,3,6),)),
        (1,3,((7,1,4,5),)),
        (1,5,((4,4,3),(3,6,3),(0,3,4))),
        (1,6,((0,4,4,3,6),)),
        (1,7,((3,6),(0,3,6))),
    ),
    (
        (0,0,((2,5,5),(3,3,3),(6,0,1,0,5))),
        (0,1,((0,0,2),(5,1))),
        (0,2,((5,3,0),(0,4))),
        (0,3,((4,4,1),(1,6))),
        (0,4,((7,0),(3,6))),
        (0,5,((7,7),(3,1,2,1))),
        (0,6,((3,6,2,1),(4,7))),
        (0,7,((4,1),(5,7))),
        (1,1,((0,7),)),
        (1,2,((2,1,4,5),(0,7,3,6))),
        (1,3,((4,1),)),
        (1,4,((5,1,3,4),)),
    ),
    (
        (0,2,((7,6,0,1),)),
        (0,5,((3,5,1,0),)),
        (0,6,((1,3,1,0),)),
        (1,1,((2,6,3),)),
        (1,2,((1,6,3),)),
        (1,3,((2,3,4),)),
        (1,5,((1,6,4,3),)),
        (1,6,((1,1,5),)),
        (1,7,((3,1,3,4),)),
    ),
    (
        (0,0,((4,2,3,5),(6,2,4))),
        (0,1,((7,2,1),(7,4,2))),
        (0,2,((5,5,2,0),(4,2,1))),
        (0,3,((1,4),(7,0,0))),
        (0,4,((1,7,1),(6,6,0))),
        (0,5,((6,0),(4,4))),
        (0,6,((4,6),(2,6,0))),
        (0,7,((2,7,2,0),(6,2,2))),
        (1,1,((1,1),)),
        (1,3,((3,5,4),(4,4))),
        (1,4,((5,6,3,4),)),
        (1,5,((3,7,5),)),
        (1,6,((1,0,4,3),)),
        (1,7,((3,7,5,4),)),
    ),
    (
        (0,6,((1,4,1,0),)),
        (1,1,((7,7,3,5),)),
        (1,2,((5,0,4,5),(4,7,3))),
        (1,3,((2,6,5),)),
        (1,4,((3,0),)),
        (1,6,((3,5),(1,2,5))),
        (1,7,((1,4,3,4),)),
    ),
    (
        (0,0,((6,1,0,3),(6,4,1,5))),
        (0,1,((6,7,1),(2,4))),
        (0,2,((0,5,0,2),(0,6,1))),
        (0,3,((4,7,1),(7,3))),
        (0,4,((2,0,2,1),(5,3))),
        (0,5,((3,0),(3,4,1))),
        (0,6,((3,7,1),)),
        (0,7,((1,2,0),)),
        (1,1,((0,6,6),)),
        (1,4,((2,4,3,4),)),
        (1,5,((4,7,4,3),(0,2,6))),
        (1,7,((0,5),(2,3,4))),
    ),
    (
        (0,1,((7,1,0),)),
        (0,3,((5,2,1,0),)),
        (0,6,((0,0,0),)),
        (0,7,((6,4),)),
        (1,1,((3,5),)),
        (1,2,((7,1,4,5),)),
        (1,3,((0,0,6),)),
        (1,4,((0,1),(0,3,6))),
        (1,5,((0,4,4,6),)),
        (1,6,((4,1,4,3),(3,0,4),(4,4,3))),
    ),
    (
        (0,0,((1,3,3,6),(3,4,4,6))),
        (0,1,((7,0),)),
        (0,2,((5,6),)),
        (0,3,((5,0),)),
        (0,4,((2,2),)),
        (0,5,((6,1),(3,6,2))),
        (0,6,((5,1),)),
        (0,7,((1,5,1),(1,0,0))),
        (1,1,((3,3,3,5),)),
        (1,2,((7,4),)),
        (1,3,((5,4,4),(1,2))),
        (1,7,((0,4,6),)),
    ),
    (
        (0,1,((5,4),)),
        (0,2,((4,3),)),
        (0,3,((0,3,2),)),
        (0,4,((0,4,0),)),
        (0,7,((6,7),)),
        (1,1,((2,1),)),
        (1,4,((5,4,4),(3,1,3))),
        (1,5,((5,1,5),)),
        (1,6,((3,1),)),
        (1,7,((5,1,4),)),
    ),
    (
        (0,0,((3,2,0,4,6),)),
        (0,2,((3,2),)),
        (0,6,((3,5),(1,6,1,0))),
        (1,1,((4,2,3),)),
        (1,2,((2,3,4),(1,1,3),(2,6))),
        (1,3,((0,7,6),(5,7,4))),
        (1,4,((1,6),)),
        (1,5,((1,0),)),
        (1,6,((3,6,5),(4,6,4,3))),
    ),
    (
        (0,0,((6,5,0,3),(6,3,1,3,6))),
        (0,1,((7,3,1),(7,7))),
        (0,2,((5,7,2,0),(0,7))),
        (0,3,((2,2),(7,5))),
        (0,4,((2,1,1),(2,4,0))),
        (0,5,((6,3),(1,3),(0,0))),
        (0,6,((0,6),)),
        (0,7,((2,2),(1,7,2,1))),
        (1,1,((5,0),)),
        (1,4,((2,5,3,4),(1,4))),
        (1,5,((5,6,5,3),(2,2,4,3))),
        (1,7,((1,0,3),(5,6,5),(7,1,3))),
    ),
    (
        (0,0,((1,5,5),)),
        (0,3,((2,7,0),)),
        (0,6,((0,1,1,0),)),
        (1,1,((6,1,3,5),)),
        (1,2,((3,5),)),
        (1,3,((1,6),(6,2,4,5))),
        (1,6,((3,7,5),(1,6,3))),
    ),
    (
        (0,0,((6,6,0,3),(4,3,4,6))),
        (0,1,((0,2),(3,1),(6,0,0))),
        (0,2,((3,0,2),(3,6),(6,5))),
        (0,3,((5,1,1),(5,3,0))),
        (0,4,((2,3,1),(1,1))),
        (0,5,((3,2),(1,4))),
        (0,6,((0,7,1),)),
        (0,7,((1,3,0),(2,0))),
        (1,2,((7,7,3),(1,2,4))),
        (1,3,((3,7),)),
        (1,4,((4,7),(6,0,3,4))),
        (1,5,((4,1,4),(2,4,5,3),(7,4,4,3))),
        (1,7,((4,1),(2,4,5))),
    ),
    (
        (0,3,((6,2),)),
        (0,6,((5,0),)),
        (1,1,((7,1),(1,3,3,5),(3,7))),
        (1,3,((4,7),(3,4,4,5))),
        (1,6,((2,1,4,3),(1,4,4),(4,7,3))),
    ),
    (
        (0,0,((7,0,5),(4,5,4,6))),
        (0,1,((7,5,2,1),(6,1))),
        (0,2,((4,0),(4,1,1))),
        (0,3,((5,6),(7,6))),
        (0,4,((2,6),(0,6,0))),
        (0,5,((6,5),(3,7,1))),
        (0,6,((5,6),)),
        (0,7,((2,6),)),
        (1,2,((5,4,4),(3,3,3))),
        (1,4,((0,4,6),(4,2,3,4))),
        (1,5,((3,0),(3,1))),
        (1,7,((2,6,3,4),(4,4,3),(5,4,4))),
    ),
    (
        (0,5,((7,4,1,0),)),
        (0,6,((0,2,1,0),)),
        (1,1,((2,3),)),
        (1,6,((2,3,4),)),
    ),
    (
        (0,0,((5,2,0,3),(7,2,4))),
        (0,1,((7,6,1),)),
        (0,2,((3,5),)),
        (0,3,((2,6),)),
        (0,4,((7,6),)),
        (0,5,((6,6),(1,6))),
        (0,6,((1,5),)),
        (0,7,((2,1),(1,4,0))),
        (1,1,((6,5,3,5),(5,1))),
        (1,2,((3,6,4,3),(5,7,5))),
        (1,3,((3,2,4,5),(1,1))),
        (1,4,((1,0),)),
        (1,5,((4,6,5),(7,7,4,3))),
        (1,6,((5,6,5),(5,0,4,3))),
        (1,7,((4,6,3),)),
    ),
    (
        (0,1,((3,2),(3,6))),
        (0,2,((4,4,1),)),
        (0,3,((5,5,0),)),
        (0,4,((2,5,0),)),
        (1,2,((4,2,5),)),
        (1,3,((5,6),)),
        (1,4,((6,4,3,4),(2,2))),
        (1,5,((2,5,5),)),
        (1,6,((5,1,5),)),
        (1,7,((2,5,5,4),)),
    ),
    (
        (0,6,((0,3,1),)),
        (0,7,((0,3),(2,3))),
        (1,1,((6,3,3,5),)),
        (1,2,((3,7),)),
        (1,3,((4,3,4,5),)),
        (1,4,((7,1),)),
        (1,5,((2,1,4),)),
        (1,6,((2,2,5,3),(7,1,4))),
    ),
    (
        (0,0,((2,7,0,3,5,6),(6,7,4,5,6),(2,0,1,3,5,6))),
        (0,1,((4,2),(6,5))),
        (0,2,((4,6),(4,7))),
        (0,3,((5,4,2,1),(1,7,0),(0,5))),
        (0,4,((3,3,1),(2,7,0))),
        (0,5,((0,4,0),(0,1))),
        (0,6,((1,7),)),
        (0,7,((0,0,0),)),
        (1,1,((5,6),)),
        (1,2,((6,2,4,5),(6,1,3))),
        (1,3,((2,4),(7,7))),
        (1,4,((1,5,3,4),)),
        (1,5,((6,0,5),)),
        (1,7,((6,2),(1,6),(6,0,5,4))),
    ),
    (
        (0,6,((5,5,0),)),
        (1,1,((6,6,3,5),(1,2,6))),
        (1,3,((4,5,4,5,6),)),
        (1,4,((4,1),(2,6,3))),
        (1,5,((3,3,4,3),)),
        (1,6,((2,6),(2,4,5))),
    ),
    (
        (0,0,((5,3,3,5,6),(7,3,4,5,6))),
        (0,1,((0,6),(6,6))),
        (0,2,((4,5,0),(5,2))),
        (0,3,((6,0),(5,7))),
        (0,4,((3,1),(1,2))),
        (0,5,((2,4),(0,7,1))),
        (0,6,((7,4),)),
        (0,7,((1,6,0),)),
        (1,1,((2,4),)),
        (1,2,((3,4,4,5,6),(1,3,3,6))),
        (1,4,((7,0,3,4),(7,4))),
        (1,5,((1,4,5),(4,2))),
        (1,7,((3,4,3,6),(2,1),(4,2,5))),
    ),
    (
        (0,6,((0,5,1,0),)),
        (1,1,((5,2,3,5),(5,4))),
        (1,3,((3,3,6),(7,2,4,5))),
        (1,4,((4,4),)),
        (1,6,((5,4,4),)),
    ),
    (
        (0,0,((5,5,3,5,6),(7,5,3,4,5))),
        (0,1,((4,1),(5,2))),
        (0,2,((7,1,0),(5,1))),
        (0,3,((6,4),)),
        (0,4,((3,5,1),(1,0))),
        (0,5,((7,5,1),(0,6),(0,2,1))),
        (0,7,((0,1,0),)),
        (1,2,((3,2,4,6),(6,5,3))),
        (1,3,((2,5),)),
        (1,5,((2,3),(6,1,3),(6,4,5))),
        (1,6,((7,4,3),)),
        (1,7,((3,2,3,4),(4,7),(6,4,5))),
    ),
    (
        (0,6,((0,4),(5,7))),
        (0,7,((3,3),)),
        (1,1,((4,6),)),
        (1,2,((5,6),)),
        (1,3,((3,6,6),)),
        (1,4,((7,7,4),)),
        (1,6,((5,7,4,3),(2,5,5))),
    ),
    (
        (0,0,((7,6,3,4,5,6),)),
        (0,1,((4,4),)),
        (0,2,((6,0),)),
        (0,3,((6,3),)),
        (0,4,((3,4,1),)),
        (0,5,((2,5),(0,3,1))),
        (0,7,((0,2),)),
        (1,1,((3,6),(2,7,3))),
        (1,2,((5,1,3),(4,3,4,6))),
        (1,3,((6,7,4,5),(6,0))),
        (1,4,((4,6),(2,7,3,4,6))),
        (1,5,((5,0),(1,3,4,3,6))),
        (1,6,((7,7),(4,2))),
        (1,7,((5,0,3),)),
    ),
    (
        (0,0,((1,7,3,4,5,6),)),
        (0,1,((2,7),)),
        (0,2,((5,4),)),
        (0,4,((1,3),)),
        (1,1,((2,5,6),(2,0,3,6))),
        (1,2,((6,3,3,5),(2,2))),
        (1,4,((6,7,3),(2,1))),
        (1,5,((1,5,5,3),)),
        (1,7,((1,5,5),(4,3,3,4,6))),
    ),
    (
        (0,3,((4,5),)),
        (0,6,((3,0),)),
        (1,1,((6,2),)),
        (1,3,((7,3,4,5),(6,1),(4,2,6))),
        (1,4,((3,4,6),)),
        (1,5,((7,1),)),
        (1,6,((6,0,5),(3,3,3))),
    ),
    (
        (0,3,((2,0),)),
        (0,4,((1,4),(3,7))),
        (0,5,((2,7),(0,5))),
        (0,7,((5,5,0),)),
        (1,1,((6,0,6),)),
        (1,2,((4,5,4,6),(6,6,3))),
        (1,4,((2,0,3,4,6),)),
        (1,5,((6,5,4,3),(2,6))),
        (1,7,((2,2,5),(4,5,3,4,6),(7,0,5,4))),
    ),
    (
        (0,3,((7,1),)),
        (0,4,((7,4),)),
        (0,7,((3,5),(5,4))),
        (1,1,((5,3,3,5,6),(3,4,6))),
        (1,3,((7,5),(1,3,6))),
        (1,4,((3,3),(3,2,6))),
        (1,6,((3,2,4,6),(6,2,4),(6,1,3))),
    ),
    (
        (0,4,((0,0),)),
        (0,7,((0,5,0),)),
        (1,1,((1,4),)),
        (1,2,((7,2,4),(5,2,3,5))),
        (1,3,((6,4,4),)),
        (1,5,((5,4),(6,3,4),(7,0,5))),
        (1,7,((7,4,5),(7,2,3,4))),
    ),
    (
        (0,7,((3,4),)),
        (1,2,((2,4),)),
        (1,3,((7,6,4,5),(6,5))),
        (1,4,((1,3,4,6),)),
        (1,6,((3,4,4,6),)),
        (1,7,((7,7),)),
    ),
    (
        (0,4,((0,7),(1,6))),
        (1,1,((3,2,6),(5,5,3))),
        (1,2,((6,7,4),)),
        (1,3,((1,5),)),
        (1,4,((5,3,4),(5,0))),
        (1,5,((5,7,5),(6,6,4,3),(6,7,6))),
        (1,6,((1,3,6),(4,3,4,6))),
        (1,7,((5,7,3),(6,7,4))),
    ),
    (
        (1,1,((6,4),(7,5,3))),
        (1,2,((2,5),)),
        (1,4,((7,3,3),(4,3,6),(6,5))),
    ),
    (
        (0,4,((7,5),)),
        (1,1,((4,3,6),)),
        (1,2,((2,7,3,6),(2,0,5,6),(7,3,4))),
        (1,3,((1,7,4,5,6),(5,1),(2,2))),
        (1,5,((5,2,4),)),
        (1,6,((6,3,3,6),(1,5,5),(4,5,6))),
        (1,7,((2,7,6),(2,0,5,6))),
    ),
    (
        (0,4,((0,1),)),
        (1,1,((1,5),)),
        (1,2,((6,0,6),)),
        (1,5,((3,2,6),)),
        (1,7,((3,3,6),(7,3,6))),
    ),
    (
        (1,1,((7,6,5,6),(4,5,5,6))),
        (1,3,((6,3,6),(7,0,6))),
        (1,4,((6,3),(4,5,6),(5,5,3,4))),
        (1,5,((2,7,3,6),(2,0,6),(6,2,4,6))),
        (1,6,((7,0,5),(6,5,3))),
    ),
    (
        (0,4,((0,2),(5,5))),
        (1,1,((7,0),)),
        (1,2,((6,4,5,6),(5,3,6))),
        (1,4,((7,5,3,4),)),
        (1,5,((5,3,3,6),)),
        (1,6,((5,2),)),
        (1,7,((6,1,3),(7,6,4))),
    ),
    (
        (1,1,((1,7,5,6),(7,2))),
        (1,3,((6,6,6),)),
        (1,4,((7,2,6),(6,6,6))),
        (1,7,((1,3,6),)),
    ),
    (
        (0,4,((0,3),(0,5))),
        (1,1,((5,7,6),)),
        (1,2,((7,6),)),
        (1,3,((7,4,6),)),
        (1,5,((7,3,3),(3,4,6))),
        (1,6,((6,6,3),(7,2,4))),
        (1,7,((6,3,6),)),
    ),
    (
        (1,2,((1,5),(5,5,3,5,6))),
        (1,3,((5,2,5),)),
        (1,4,((7,6,6),)),
        (1,6,((2,0,6),)),
        (1,7,((1,7,4,6),(5,3,5))),
    ),
    (
        (1,1,((6,7,6),)),
        (1,2,((7,5,5,6),(1,7,6))),
        (1,3,((2,0,6),)),
        (1,4,((5,7,6),(5,2,6))),
        (1,5,((4,3,6),)),
        (1,6,((6,7),)),
    ),
    (
        (1,2,((7,0,6),)),
        (1,4,((1,7,6),)),
        (1,7,((6,5),)),
    ),
    (
        (1,1,((7,3,6),)),
        (1,3,((2,7,6),)),
        (1,4,((6,1),(6,2,6))),
        (1,5,((7,6),(4,5,6),(5,5,6),(7,5,6))),
        (1,6,((6,4,6),)),
        (1,7,((5,5,6),)),
    ),
    (
        (1,5,((7,2,6),)),
        (1,6,((7,6),(2,7,6),(5,3,6))),
        (1,7,((7,5,6),)),
    ),
    (
        (1,7,((6,6,6),)),
    ),
    (
        (1,3,((5,3,6),)),
        (1,5,((1,7,6),)),
        (1,6,((1,7,6),(7,5,6))),
        (1,7,((5,2,6),)),
    ),
    (),
    (
        (1,3,((5,5,6),)),
        (1,6,((7,3,6),)),
    ),
    (
        (1,6,((5,5,6),)),
    ),
)
XP, XM, ZH, YP, YM, ZL, CORE = range(7)


def place():
    row, col = lax.axis_index("row"), lax.axis_index("col")
    return col // 2, lax.rem(col, 2), lax.rem(row // 2, 4), row // 8, lax.rem(row, 2)


def device(x, zh, y, zl, core):
    return (zl * 8 + y * 2 + core, x * 2 + zh)


def neighbours(x, zh, y, zl, core):
    def turn(a, by):
        return lax.rem(a + by, 4)

    return {
        XP: device(turn(x, 1), zh, y, zl, core),
        XM: device(turn(x, 3), zh, y, zl, core),
        ZH: device(x, 1 - zh, y, zl, core),
        YP: device(x, zh, turn(y, 1), zl, core),
        YM: device(x, zh, turn(y, 3), zl, core),
        ZL: device(x, zh, y, 1 - zl, core),
        CORE: device(x, zh, y, zl, 1 - core),
    }


def flip(a, b):
    return a + b - 2 * a * b


class Place:
    def __init__(self):
        self.coordinates = x, zh, y, zl, core = place()
        self.core = core
        self.row_root = (2 * zl + y // 2, lax.rem(y, 2))
        self.col_root = (2 * lax.rem(x, 2) + zh, x // 2)
        self.row_place = lax.rem(x - self.row_root[0] + 4, 4) + 4 * flip(zh, self.row_root[1])
        self.col_place = lax.rem(y - self.col_root[0] + 4, 4) + 4 * flip(zl, self.col_root[1])

    def row_shard(self, source):
        return lax.rem(self.row_root[0] + source % 4, 4) * 2 + flip(self.row_root[1], source // 4)

    def col_shard(self, source):
        return lax.rem(self.coordinates[0] + source % 4, 4) * 2 + flip(self.coordinates[1], source // 4)


def dot(lhs, rhs):
    return lax.dot_general(lhs, rhs, (((1,), (1,)), ((), ())), preferred_element_type=jnp.float32)


def clear_diagonal(block):
    same = lax.broadcasted_iota(jnp.int32, block.shape, 0) == lax.broadcasted_iota(jnp.int32, block.shape, 1)
    return jnp.where(same, 0.0, block.astype(jnp.float32)).astype(block.dtype)


def gather_kernel(
    pattern_hbm, weights_hbm, left, right, pattern_ref, weights_ref, in_sems, send_sems, row_sems, col_sems, core_sem
):
    loads = [
        pltpu.make_async_copy(weights_hbm, weights_ref, in_sems.at[0]),
        pltpu.make_async_copy(pattern_hbm, pattern_ref, in_sems.at[1]),
    ]
    for load in loads:
        load.start()
    reads, bins = weights_ref.shape
    section_count = pattern_ref.shape[1]
    bin_tile = bins // section_count
    piece = reads // CHUNKS
    x, zh, y, zl, core = place()
    near = neighbours(x, zh, y, zl, core)
    barrier = pltpu.get_barrier_semaphore()
    for target in near.values():
        pl.semaphore_signal(barrier, inc=1, device_id=target, device_id_type=MESH)
    own = pl.multiple_of((x * 2 + zh) * reads, reads)
    for load in loads:
        load.wait()
    for section in range(section_count):
        part = pl.ds(section * bin_tile, bin_tile)
        keep = pattern_ref[0, section].astype(jnp.float32)
        left[pl.ds(own, reads), part] = (weights_ref[:, part].astype(jnp.float32) * keep).astype(left.dtype)
    pl.semaphore_wait(barrier, len(near))

    here = Place()
    row_place, col_place = here.row_place, here.col_place
    row_source = [here.row_shard(s) for s in range(8)]
    col_source = [here.col_shard(s) for s in range(8)]
    row_tile = [pl.multiple_of(a * reads, reads) for a in row_source]
    col_tile = [pl.multiple_of((core * 8 + a) * reads, reads) for a in col_source]

    def in_left(s, c):
        return left.at[pl.ds(row_tile[s] + c * piece, piece)]

    def in_right(s, c):
        return right.at[pl.ds(col_tile[s] + c * piece, piece)]

    def copy(src, dst, way, recv_sem):
        return pltpu.make_async_remote_copy(
            src_ref=src, dst_ref=dst, send_sem=send_sems.at[way], recv_sem=recv_sem, device_id=near[way], device_id_type=MESH
        )

    def handle(kind, role, s, c, ways):
        row_sem = row_sems.at[row_source[s], c]
        col_sem = col_sems.at[col_source[s], c]
        if kind == 0:
            src = in_left(s, c)
            if s != role:
                copy(src, src, XP, row_sem).wait_recv()
        else:
            src = in_right(s, c)
            copy(src, src, YP, col_sem).wait_recv()
        for way in ways:
            if way <= ZH:
                copy(src, src, way, row_sem).start()
            elif way <= ZL:
                copy(src, in_right(s, c), way, col_sem).start()
            else:
                part = c * UNITS // CHUNKS
                start = part * (reads // UNITS)
                held = (left if kind == 0 else right).at[pl.ds((row_tile if kind == 0 else col_tile)[s] + start, reads // UNITS)]
                target = right.at[pl.ds(col_tile[s] + start, reads // UNITS)]
                copy(held, target, CORE, core_sem).start()
                if kind == 0:
                    target[...] = held[...]

    sent = {}

    def run_slot(slot):
        for kind, role, entries in SLOTS[slot]:
            for entry in entries:
                for way in entry[2:]:
                    at = (0 if way <= ZH else 1, role, way)
                    sent[at] = sent.get(at, 0) + 1

            @pl.when((row_place if kind == 0 else col_place) == role)
            def _(kind=kind, role=role, entries=entries):
                for entry in entries:
                    handle(kind, role, entry[0], entry[1], entry[2:])

    def dispatch(slot, low, high):
        if high - low == 1:
            run_slot(low)
            return
        middle = (low + high) // 2

        @pl.when(slot < middle)
        def _():
            dispatch(slot, low, middle)

        @pl.when(slot >= middle)
        def _():
            dispatch(slot, middle, high)

    @pl.loop(0, len(SLOTS))
    def _(slot):
        dispatch(slot, 0, len(SLOTS))

    for (kind, role, way), count in sorted(sent.items()):

        @pl.when((row_place if kind == 0 else col_place) == role)
        def _(way=way, count=count):
            block = right.at[pl.ds(0, 8 * reads if way == CORE else count * piece)]
            copy(block, block, way, core_sem).wait_send()
            if way == CORE:
                copy(block, block, way, core_sem).wait_recv()


def gather(tile_pattern, weights):
    reads, bins = weights.shape
    return pl.pallas_call(
        gather_kernel,
        out_shape=(pltpu.VMEM((8 * reads, bins), weights.dtype), pltpu.VMEM((16 * reads, bins), weights.dtype)),
        in_specs=[pl.BlockSpec(memory_space=pltpu.HBM), pl.BlockSpec(memory_space=pltpu.HBM)],
        out_specs=(pl.BlockSpec(memory_space=pltpu.VMEM),) * 2,
        scratch_shapes=[
            pltpu.SMEM(tile_pattern.shape, tile_pattern.dtype),
            pltpu.VMEM(weights.shape, weights.dtype),
            pltpu.SemaphoreType.DMA((2,)),
            pltpu.SemaphoreType.DMA((7,)),
            pltpu.SemaphoreType.DMA((8, CHUNKS)),
            pltpu.SemaphoreType.DMA((8, CHUNKS)),
            pltpu.SemaphoreType.DMA,
        ],
        compiler_params=pltpu.CompilerParams(collective_id=0, has_side_effects=True, vmem_limit_bytes=8 << 20),
        name="gather",
    )(*[pltpu.with_memory_space_constraint(a, pltpu.HBM) for a in (tile_pattern, weights)])


def product_kernel(scale, left, right, out, full, stage, sems):
    row, col = lax.axis_index("row"), lax.axis_index("col")
    slots, _, tile = stage.shape
    section_count = full.shape[1]
    bin_tile = left.shape[1] // section_count
    rows, cols = left.shape[0] // tile, right.shape[0] // tile

    def tile_at(index):
        return pl.ds(pl.multiple_of(index * tile, tile), tile)

    def write(j, slot):
        return pltpu.make_async_copy(stage.at[slot], out.at[:, tile_at(j)], sems.at[slot])

    for j in range(cols):
        for s in range(section_count):
            part = jnp.abs(right[pl.ds(j * tile, tile), pl.ds(s * bin_tile, bin_tile)]).reshape(-1, 16, bin_tile)
            top = jnp.max(jnp.max(part, axis=0).astype(jnp.float32))
            full[j, s] = (top > 0.0).astype(jnp.int32)

    @pl.loop(0, cols)
    def _(j):
        slot = lax.rem(j, slots)

        @pl.when(j >= slots)
        def _():
            write(j - slots, slot).wait()

        case = full[j, 0] + 2 * full[j, 1]

        def put(part):
            stage[slot] = (dot(left[:, part], right[tile_at(j), part]) * scale).astype(stage.dtype)

        @pl.when(case == 0)
        def _():
            stage[slot] = jnp.zeros(stage.shape[1:], stage.dtype)

        @pl.when(case == 1)
        def _():
            put(pl.ds(0, bin_tile))

        @pl.when(case == 2)
        def _():
            put(pl.ds(bin_tile, bin_tile))

        @pl.when(case == 3)
        def _():
            put(pl.ds(0, 2 * bin_tile))

        i = col * cols + j - row * rows

        @pl.when(jnp.logical_and(i >= 0, i < rows))
        def _():
            stage[slot, tile_at(i), :] = clear_diagonal(stage[slot, tile_at(i), :])

        write(j, slot).start()

    for j in range(cols - slots, cols):
        write(j, j % slots).wait()


def product(left, right, section_count):
    rows, cols = left.shape[0], right.shape[0]
    tile = rows // 8
    slots = 8

    def kernel(*refs):
        product_kernel(1.0 / math.sqrt(left.shape[1]), *refs)

    return pl.pallas_call(
        kernel,
        out_shape=jax.ShapeDtypeStruct((rows, cols), left.dtype),
        in_specs=[pl.BlockSpec(memory_space=pltpu.VMEM)] * 2,
        out_specs=pl.BlockSpec(memory_space=pl.ANY),
        scratch_shapes=[
            pltpu.SMEM((cols // tile, section_count), jnp.int32),
            pltpu.VMEM((slots, rows, tile), left.dtype),
            pltpu.SemaphoreType.DMA((slots,)),
        ],
        compiler_params=pltpu.CompilerParams(vmem_limit_bytes=24 << 20),
        name="product",
    )(left, right)


def shards(weights, tile_pattern):
    return product(*gather(tile_pattern, weights), tile_pattern.shape[1])


def solution(mesh):
    return jax.shard_map(
        shards,
        mesh=mesh,
        in_specs=(P(("row", "col"), None), P(("row", "col"), None)),
        out_specs=P("row", "col"),
        check_vma=False,
    )
```

time: 329 us -> 72 us (0.22)
  the two profiles are of different devices: /device:TPU:7 before, /device:TPU:35 now
where the time goes in v3:
time: 72 us; the launch traced here: 71.9 us
  Pallas kernels  71.7 us (100%)
    pallas_call x1, Pallas kernels, gather(): pl.pallas_call(gather_kernel, out_shape=(pltpu.VMEM((8 * reads, bins), we...  54.8 us
    pallas_call x1, Pallas kernels, product(): pl.pallas_call(kernel, out_shape=jax.ShapeDtypeStruct((rows, cols), left....  16.9 us

profile of v3, /device:TPU:35, one launch (start us, length us, event | category | flops | bytes accessed | tf_op | source)
XLA Modules:
  0.0 71.9 jit_solution(15262328164869218613)
XLA Ops:
  0.0 54.8 %gather.1 = (bf16[2048,1024]{1,0:T(8,128)(2,1)S(1)}, bf16[4096,1024]{1,0:T(8,128)(2,1)S(1)}) custom-call(s32[1,2]{1,0:T(1,128)} %pattern_hbm.1, bf16[256,1024]{1,0:T(8,128)(2,1)} %weights_hbm.1), custom_call_target="tpu_custom_call" | custom-call | tf_op jit(solution)/shard_map/gather/pallas_call | solution.py:934
  54.8 16.9 %product.1 = bf16[2048,4096]{1,0:T(8,128)(2,1)} custom-call(bf16[2048,1024]{1,0:T(8,128)(2,1)S(1)} %get-tuple-element.7.refs_0_, bf16[4096,1024]{1,0:T(8,128)(2,1)S(1)} %get-tuple-element.8.refs_1_), custom_call_target="tpu_custom_call" | custom-call | tf_op jit(solution)/shard_map/product/pallas_call | solution.py:1021

commit v4 on v3

--- a/solution.py
+++ b/solution.py
@@ -25,7 +25,14 @@
     (),
     (),
     (),
-    (
+    (),
+    (),
+    (),
+    (),
+    (),
+    (),
+    (
+        (1,4,((0,0,3),)),
         (0,0,((3,0,0,4),(1,0,1,3))),
         (0,1,((2,0),(0,1))),
         (0,2,((1,0,2),(3,1,2))),
@@ -34,29 +41,38 @@
         (0,5,((4,0,0,2),)),
         (0,6,((7,0,1,2),)),
         (0,7,((6,0,0),)),
-        (1,4,((0,0,3),)),
-    ),
-    (
+    ),
+    (
+        (1,3,((0,1,4),)),
+        (0,5,((6,2,1),)),
+        (0,6,((5,2),)),
+        (0,7,((4,2,1,2),)),
+    ),
+    (
+        (1,1,((0,3,3),)),
         (0,0,((4,0,1,3,5),)),
         (0,1,((5,0,0,1),)),
-        (0,5,((6,2,1),)),
-        (0,6,((5,2),(2,0,1))),
-        (0,7,((4,2,1,2),(3,0,0))),
-        (1,1,((0,3,3),)),
-        (1,3,((0,1,4),)),
-    ),
-    (
+        (0,6,((2,0,1),)),
+        (0,7,((3,0,0),)),
+    ),
+    (
+        (0,2,((6,1,0),)),
+        (0,3,((7,2,1),)),
+        (0,5,((1,1,0),)),
+    ),
+    (
+        (1,4,((0,6,3,4),)),
         (0,0,((3,1,4),(1,1,5))),
         (0,1,((2,2,1,2),)),
-        (0,2,((6,1,0),(1,1,0))),
-        (0,3,((7,2,1),(0,1,1))),
+        (0,2,((1,1,0),)),
+        (0,3,((0,1,1),)),
         (0,4,((5,1,1,2),)),
-        (0,5,((1,1,0),(4,1,0))),
+        (0,5,((4,1,0),)),
         (0,6,((7,1),)),
         (0,7,((6,1,0),)),
-        (1,4,((0,6,3,4),)),
-    ),
-    (
+    ),
+    (
+        (1,3,((0,2,4,5),)),
         (0,1,((0,3,0),)),
         (0,2,((3,3,1,2),)),
         (0,3,((2,3,0),)),
@@ -64,101 +80,136 @@
         (0,5,((6,4,1,2),)),
         (0,6,((5,3,0),)),
         (0,7,((4,3,2),)),
-        (1,3,((0,2,4,5),)),
-    ),
-    (
+    ),
+    (),
+    (
+        (1,1,((0,5,3,5),)),
         (0,0,((4,1,1,3),)),
         (0,1,((5,3,0),)),
         (0,2,((6,2,1),)),
-        (0,3,((7,4,0,1),)),
         (0,5,((1,2,0),)),
         (0,6,((2,1,1),)),
         (0,7,((3,1),)),
-        (1,1,((0,5,3,5),)),
-    ),
-    (
+    ),
+    (
+        (0,3,((7,4,0,1),)),
+    ),
+    (
+        (1,4,((0,7,3,4),)),
         (0,0,((3,5,0,5),(1,2,1,5))),
         (0,1,((2,3),(0,4))),
         (0,2,((1,2),(3,4,1,2))),
         (0,3,((0,2,1),(2,4,0))),
         (0,4,((5,2,1),(7,3,0))),
-        (0,5,((4,2),(6,7,1))),
-        (0,6,((7,2),(5,4))),
-        (0,7,((6,3,0),(4,4,1))),
+        (0,5,((4,2),)),
+        (0,6,((7,2),)),
+        (0,7,((6,3,0),)),
+    ),
+    (
         (1,3,((0,4,4),)),
-        (1,4,((0,7,3,4),)),
+        (0,5,((6,7,1),)),
+        (0,6,((5,4),)),
+        (0,7,((4,4,1),)),
     ),
     (
         (0,0,((4,4,1,3),)),
         (0,1,((5,5,0),)),
+        (0,6,((2,3,1),)),
+        (0,7,((3,2,0,1),)),
+    ),
+    (
+        (1,1,((1,0,3),)),
+        (1,2,((0,1,4,5),)),
+        (1,5,((0,0,5,3),)),
         (0,2,((6,3,1),)),
         (0,3,((7,7,0,1),)),
         (0,5,((1,5,1),)),
-        (0,6,((2,3,1),)),
-        (0,7,((3,2,0,1),)),
-        (1,1,((1,0,3),)),
-        (1,2,((0,1,4,5),)),
-        (1,5,((0,0,5,3),)),
-    ),
-    (
+    ),
+    (
+        (1,2,((0,3,3,5),)),
         (0,0,((3,6,5),(1,4,1,4))),
-        (0,1,((2,5),(0,5,0))),
-        (0,2,((1,3,0,2),(3,7,1))),
-        (0,3,((0,4,1,2),(2,5,0))),
-        (0,4,((5,4,2),(7,7,0))),
-        (0,5,((4,3,0,2),(7,0,1))),
-        (0,6,((7,3,2),(4,0,0))),
-        (0,7,((6,5,0,2),(4,5))),
-        (1,2,((0,3,3,5),)),
+        (0,1,((2,5),)),
+        (0,2,((1,3,0,2),)),
+        (0,3,((0,4,1,2),)),
+        (0,4,((5,4,2),)),
+        (0,5,((4,3,0,2),)),
+        (0,6,((7,3,2),)),
+        (0,7,((6,5,0,2),)),
+    ),
+    (
         (1,3,((3,0,4,5),)),
         (1,4,((4,0,3,4),)),
-    ),
-    (
+        (0,1,((0,5,0),)),
+        (0,2,((3,7,1),)),
+        (0,3,((2,5,0),)),
+        (0,4,((7,7,0),)),
+        (0,5,((7,0,1),)),
+        (0,6,((4,0,0),)),
+        (0,7,((4,5),)),
+    ),
+    (),
+    (
+        (1,1,((4,0,3),)),
+        (1,5,((0,6),)),
+        (1,7,((0,6,5,4),)),
         (0,0,((4,6,0,4),)),
         (0,1,((5,6,0,1),)),
         (0,2,((6,4),)),
         (0,5,((1,7,1),)),
         (0,6,((2,4,0),)),
         (0,7,((3,6,0,1),)),
-        (1,1,((4,0,3),)),
-        (1,5,((0,6),)),
-        (1,7,((0,6,5,4),)),
-    ),
-    (
+    ),
+    (
+        (1,2,((0,2,4),)),
+        (0,3,((4,2,0,1),)),
+    ),
+    (
+        (1,2,((0,5,3),)),
+        (1,4,((1,1,3,4),)),
         (0,0,((3,7,5),(1,6,3))),
         (0,1,((2,6,1,2),(0,7))),
         (0,2,((1,4,2),(0,0,1,2))),
-        (0,3,((4,2,0,1),(0,6,1,2),(6,1,0))),
+        (0,3,((0,6,1,2),(6,1,0))),
         (0,4,((5,6,1),(6,0,0,2))),
         (0,5,((4,5,0,2),)),
         (0,6,((7,5,2),)),
         (0,7,((6,6,0),)),
-        (1,2,((0,2,4),(0,5,3))),
-        (1,4,((1,1,3,4),)),
+    ),
+    (
+        (1,3,((3,1,4,5),)),
+        (0,5,((2,0,1),)),
+        (0,6,((1,1,0),)),
+        (0,7,((4,6,1,2),)),
     ),
     (
         (0,0,((4,7,0,1,3),)),
         (0,1,((5,7,0,1),)),
-        (0,5,((2,0,1),)),
-        (0,6,((1,1,0),(2,5,0))),
-        (0,7,((4,6,1,2),(3,7,1))),
-        (1,3,((3,1,4,5),)),
-    ),
-    (
-        (0,0,((2,1,0,4),(5,0,1,4))),
-        (0,1,((3,3,1,2),)),
-        (0,2,((6,6,0),(1,5,0))),
-        (0,3,((4,3,1),(0,7,1,2))),
-        (0,4,((5,7,1),)),
-        (0,5,((2,2,0,1),(4,6))),
-        (0,6,((7,6,1,2),)),
-        (0,7,((5,3,0),)),
+        (0,6,((2,5,0),)),
+        (0,7,((3,7,1),)),
+    ),
+    (
         (1,1,((4,1,3),)),
         (1,2,((0,4,4,5),)),
         (1,5,((0,7,5,3),)),
         (1,7,((0,7),)),
-    ),
-    (
+        (0,2,((6,6,0),)),
+        (0,3,((4,3,1),)),
+        (0,5,((2,2,0,1),)),
+    ),
+    (
+        (0,0,((2,1,0,4),(5,0,1,4))),
+        (0,1,((3,3,1,2),)),
+        (0,2,((1,5,0),)),
+        (0,3,((0,7,1,2),)),
+        (0,4,((5,7,1),)),
+        (0,5,((4,6),)),
+        (0,6,((7,6,1,2),)),
+        (0,7,((5,3,0),)),
+    ),
+    (
+        (1,2,((1,0,3,5),)),
+        (1,4,((3,5,3,4),)),
+        (1,6,((0,0,3),)),
         (0,1,((3,0,0),)),
         (0,2,((7,2,1),)),
         (0,3,((1,1),)),
@@ -166,70 +217,99 @@
         (0,5,((2,1,1),)),
         (0,6,((4,1,0),)),
         (0,7,((4,7),)),
+    ),
+    (
         (1,1,((0,1),)),
-        (1,2,((1,0,3,5),)),
-        (1,4,((3,5,3,4),)),
-        (1,6,((0,0,3),(0,1,4,3))),
-    ),
-    (
+        (1,6,((0,1,4,3),)),
+    ),
+    (
+        (1,1,((4,4,3,5),)),
+        (1,3,((1,4,4,5),)),
         (0,0,((7,1,4),)),
         (0,1,((4,0,0),)),
         (0,2,((6,7,0,1),)),
         (0,6,((2,7,0),)),
-        (1,1,((4,4,3,5),)),
+    ),
+    (
         (1,2,((3,0,4),)),
-        (1,3,((1,4,4,5),(0,3))),
+        (1,3,((0,3),)),
         (1,5,((4,0),)),
         (1,7,((4,0,4),)),
     ),
     (
+        (1,2,((4,0,3),)),
+        (1,4,((1,2,3,4),)),
         (0,0,((2,3,4,5),(2,2,1,3))),
         (0,1,((6,2,1),(3,5,0,2))),
         (0,2,((1,6,0,2),(0,1,2))),
         (0,3,((1,0),(1,3,0))),
         (0,4,((6,2,1),(6,1,0))),
-        (0,5,((4,7,0),(2,3,1))),
-        (0,6,((7,7),(1,2,0))),
-        (0,7,((4,0),(5,0))),
-        (1,2,((4,0,3),)),
-        (1,4,((1,2,3,4),)),
+        (0,5,((4,7,0),)),
+        (0,6,((7,7),)),
+        (0,7,((4,0),)),
+    ),
+    (
         (1,6,((0,6,5),)),
-    ),
-    (
+        (0,5,((2,3,1),)),
+        (0,6,((1,2,0),)),
+        (0,7,((5,0),)),
+    ),
+    (
+        (1,5,((0,5,4,3),)),
+        (1,7,((0,2,3,4),)),
         (0,0,((5,1,0,1,5),)),
         (0,1,((6,4,1),)),
-        (0,2,((7,0,0,1),)),
         (0,3,((6,5,1,0),)),
         (0,6,((1,0,1,0),)),
         (0,7,((0,4,0),)),
+    ),
+    (
         (1,1,((0,0,3),(0,2,6),(1,6,3,5))),
         (1,2,((3,1,4),)),
         (1,3,((4,6,4),(0,5))),
-        (1,5,((0,5,4,3),(1,1,5))),
-        (1,7,((0,2,3,4),(1,1,4))),
-    ),
-    (
+        (1,5,((1,1,5),)),
+        (1,7,((1,1,4),)),
+        (0,2,((7,0,0,1),)),
+    ),
+    (
+        (1,6,((0,3,4,3),)),
         (0,0,((7,4,0,3),(5,6,1,5))),
-        (0,1,((3,4,1),(4,6,0))),
-        (0,2,((1,7),(7,4))),
-        (0,3,((4,0),(6,6,0))),
-        (0,4,((6,4,1),(6,3,0))),
+        (0,1,((3,4,1),)),
+        (0,2,((1,7),)),
+        (0,3,((4,0),)),
+        (0,4,((6,4,1),)),
         (0,5,((7,1,2),)),
-        (0,6,((4,2),(4,3))),
-        (0,7,((2,4,0),(5,1,1))),
+        (0,6,((4,2),)),
+        (0,7,((2,4,0),)),
+    ),
+    (
         (1,4,((3,6,3,4),)),
-        (1,6,((0,3,4,3),)),
+        (0,1,((4,6,0),)),
+        (0,2,((7,4),)),
+        (0,3,((6,6,0),)),
+        (0,4,((6,3,0),)),
+        (0,6,((4,3),)),
+        (0,7,((5,1,1),)),
     ),
     (
         (0,5,((2,6,0,1),(7,6,1))),
-        (0,6,((3,1,1),)),
+    ),
+    (
         (1,1,((0,4),(4,7,3,5))),
         (1,2,((4,1,3,5),)),
         (1,3,((2,1,4),(0,6))),
         (1,6,((0,7,5),)),
         (1,7,((0,0),)),
-    ),
-    (
+        (0,6,((3,1,1),)),
+    ),
+    (
+        (1,3,((1,0),)),
+        (1,5,((3,5,5),(0,1))),
+        (1,7,((3,5,5,4),)),
+    ),
+    (
+        (1,2,((1,4),)),
+        (1,4,((3,7,3,4),)),
         (0,0,((2,4,0,5),(2,6,1,3,4))),
         (0,1,((6,3,1),(4,7))),
         (0,2,((5,0,2),(7,3,0,1),(0,2,1,2))),
@@ -238,21 +318,25 @@
         (0,5,((7,2),)),
         (0,6,((4,4,1),)),
         (0,7,((1,1,0),(0,6,0,1))),
-        (1,2,((1,4),)),
-        (1,3,((1,0),)),
-        (1,4,((3,7,3,4),)),
-        (1,5,((3,5,5),(0,1))),
-        (1,7,((3,5,5,4),)),
-    ),
-    (
-        (0,0,((5,4,0,1,4,5),)),
+    ),
+    (
+        (1,6,((4,0),)),
         (0,1,((4,3,1),)),
         (0,5,((3,3,1),)),
-        (0,6,((4,5),(3,3))),
+        (0,6,((4,5),)),
         (0,7,((5,2,2),)),
+    ),
+    (
         (1,2,((4,4,3),)),
-        (1,6,((4,0),)),
         (1,7,((3,0,3,4),)),
+        (0,0,((5,4,0,1,4,5),)),
+        (0,6,((3,3),)),
+    ),
+    (
+        (1,1,((2,2,5),(3,0))),
+        (1,3,((5,0,4),(4,0))),
+        (1,5,((1,2,3),)),
+        (1,7,((0,1,3),(1,2,5))),
     ),
     (
         (0,0,((7,7,0,3),(5,7,4))),
@@ -263,84 +347,112 @@
         (0,5,((7,3),(1,0))),
         (0,6,((3,2,2),)),
         (0,7,((2,5,0),(0,7,1))),
-        (1,1,((2,2,5),(3,0))),
-        (1,3,((5,0,4),(4,0))),
-        (1,5,((1,2,3),)),
-        (1,7,((0,1,3),(1,2,5))),
-    ),
-    (
+    ),
+    (
+        (1,2,((0,6,4),(4,6,5))),
+        (1,4,((2,3,4),)),
         (0,1,((2,1),)),
         (0,2,((7,7),)),
         (0,3,((6,7),)),
         (0,4,((6,5,0),)),
         (0,6,((2,2,0),)),
         (0,7,((5,6,1),)),
-        (1,2,((0,6,4),(4,6,5))),
-        (1,4,((2,3,4),(0,2,3),(0,5))),
+    ),
+    (
+        (1,4,((0,2,3),(0,5))),
         (1,6,((0,5,3),(0,2,6))),
     ),
     (
-        (0,1,((4,5,1,0),)),
-        (0,2,((7,5,0,1),)),
-        (0,6,((3,4,1),)),
         (1,1,((3,1),(7,4,3,5))),
         (1,2,((0,0,3,6),)),
         (1,3,((7,1,4,5),)),
-        (1,5,((4,4,3),(3,6,3),(0,3,4))),
+        (1,5,((4,4,3),)),
+        (0,2,((7,5,0,1),)),
+        (0,6,((3,4,1),)),
+    ),
+    (
+        (1,5,((3,6,3),(0,3,4))),
         (1,6,((0,4,4,3,6),)),
         (1,7,((3,6),(0,3,6))),
-    ),
-    (
+        (0,1,((4,5,1,0),)),
+    ),
+    (
+        (1,1,((0,7),)),
+        (1,3,((4,1),)),
+        (1,4,((5,1,3,4),)),
         (0,0,((2,5,5),(3,3,3),(6,0,1,0,5))),
         (0,1,((0,0,2),(5,1))),
         (0,2,((5,3,0),(0,4))),
         (0,3,((4,4,1),(1,6))),
         (0,4,((7,0),(3,6))),
         (0,5,((7,7),(3,1,2,1))),
-        (0,6,((3,6,2,1),(4,7))),
-        (0,7,((4,1),(5,7))),
-        (1,1,((0,7),)),
+        (0,6,((3,6,2,1),)),
+        (0,7,((4,1),)),
+    ),
+    (
         (1,2,((2,1,4,5),(0,7,3,6))),
-        (1,3,((4,1),)),
-        (1,4,((5,1,3,4),)),
-    ),
-    (
-        (0,2,((7,6,0,1),)),
+        (0,6,((4,7),)),
+        (0,7,((5,7),)),
+    ),
+    (
+        (1,2,((1,6,3),)),
+        (1,6,((1,1,5),)),
+        (1,7,((3,1,3,4),)),
         (0,5,((3,5,1,0),)),
         (0,6,((1,3,1,0),)),
+    ),
+    (
         (1,1,((2,6,3),)),
-        (1,2,((1,6,3),)),
         (1,3,((2,3,4),)),
         (1,5,((1,6,4,3),)),
-        (1,6,((1,1,5),)),
-        (1,7,((3,1,3,4),)),
-    ),
-    (
-        (0,0,((4,2,3,5),(6,2,4))),
-        (0,1,((7,2,1),(7,4,2))),
-        (0,2,((5,5,2,0),(4,2,1))),
-        (0,3,((1,4),(7,0,0))),
-        (0,4,((1,7,1),(6,6,0))),
-        (0,5,((6,0),(4,4))),
-        (0,6,((4,6),(2,6,0))),
-        (0,7,((2,7,2,0),(6,2,2))),
-        (1,1,((1,1),)),
-        (1,3,((3,5,4),(4,4))),
-        (1,4,((5,6,3,4),)),
+        (0,2,((7,6,0,1),)),
+    ),
+    (
+        (1,3,((3,5,4),)),
         (1,5,((3,7,5),)),
         (1,6,((1,0,4,3),)),
+        (0,0,((4,2,3,5),(6,2,4))),
+        (0,1,((7,2,1),)),
+        (0,2,((5,5,2,0),)),
+        (0,3,((1,4),)),
+        (0,4,((1,7,1),)),
+        (0,5,((6,0),(4,4))),
+        (0,6,((4,6),)),
+        (0,7,((2,7,2,0),)),
+    ),
+    (
+        (1,1,((1,1),)),
+        (1,3,((4,4),)),
+        (1,4,((5,6,3,4),)),
         (1,7,((3,7,5,4),)),
-    ),
-    (
+        (0,1,((7,4,2),)),
+        (0,2,((4,2,1),)),
+        (0,3,((7,0,0),)),
+        (0,4,((6,6,0),)),
+        (0,6,((2,6,0),)),
+        (0,7,((6,2,2),)),
+    ),
+    (
+        (1,2,((5,0,4,5),)),
+        (1,4,((3,0),)),
+        (1,6,((3,5),)),
+    ),
+    (
+        (1,1,((7,7,3,5),)),
+        (1,2,((4,7,3),)),
+        (1,3,((2,6,5),)),
+        (1,6,((1,2,5),)),
+        (1,7,((1,4,3,4),)),
         (0,6,((1,4,1,0),)),
-        (1,1,((7,7,3,5),)),
-        (1,2,((5,0,4,5),(4,7,3))),
-        (1,3,((2,6,5),)),
-        (1,4,((3,0),)),
-        (1,6,((3,5),(1,2,5))),
-        (1,7,((1,4,3,4),)),
-    ),
-    (
+    ),
+    (
+        (1,1,((0,6,6),)),
+        (1,7,((0,5),)),
+    ),
+    (
+        (1,4,((2,4,3,4),)),
+        (1,5,((4,7,4,3),(0,2,6))),
+        (1,7,((2,3,4),)),
         (0,0,((6,1,0,3),(6,4,1,5))),
         (0,1,((6,7,1),(2,4))),
         (0,2,((0,5,0,2),(0,6,1))),
@@ -349,24 +461,31 @@
         (0,5,((3,0),(3,4,1))),
         (0,6,((3,7,1),)),
         (0,7,((1,2,0),)),
-        (1,1,((0,6,6),)),
-        (1,4,((2,4,3,4),)),
-        (1,5,((4,7,4,3),(0,2,6))),
-        (1,7,((0,5),(2,3,4))),
-    ),
-    (
+    ),
+    (
+        (1,2,((7,1,4,5),)),
+        (1,4,((0,1),)),
+        (1,6,((4,1,4,3),)),
         (0,1,((7,1,0),)),
         (0,3,((5,2,1,0),)),
+        (0,7,((6,4),)),
+    ),
+    (
+        (1,1,((3,5),)),
+        (1,3,((0,0,6),)),
+        (1,4,((0,3,6),)),
+        (1,5,((0,4,4,6),)),
+        (1,6,((3,0,4),(4,4,3))),
         (0,6,((0,0,0),)),
-        (0,7,((6,4),)),
-        (1,1,((3,5),)),
-        (1,2,((7,1,4,5),)),
-        (1,3,((0,0,6),)),
-        (1,4,((0,1),(0,3,6))),
-        (1,5,((0,4,4,6),)),
-        (1,6,((4,1,4,3),(3,0,4),(4,4,3))),
-    ),
-    (
+    ),
+    (
+        (1,1,((3,3,3,5),)),
+        (1,2,((7,4),)),
+        (1,3,((5,4,4),(1,2))),
+        (0,7,((1,5,1),)),
+    ),
+    (
+        (1,7,((0,4,6),)),
         (0,0,((1,3,3,6),(3,4,4,6))),
         (0,1,((7,0),)),
         (0,2,((5,6),)),
@@ -374,81 +493,118 @@
         (0,4,((2,2),)),
         (0,5,((6,1),(3,6,2))),
         (0,6,((5,1),)),
-        (0,7,((1,5,1),(1,0,0))),
-        (1,1,((3,3,3,5),)),
-        (1,2,((7,4),)),
-        (1,3,((5,4,4),(1,2))),
-        (1,7,((0,4,6),)),
-    ),
-    (
+        (0,7,((1,0,0),)),
+    ),
+    (
+        (1,1,((2,1),)),
+        (1,4,((5,4,4),)),
+        (1,5,((5,1,5),)),
+        (1,7,((5,1,4),)),
         (0,1,((5,4),)),
         (0,2,((4,3),)),
         (0,3,((0,3,2),)),
         (0,4,((0,4,0),)),
         (0,7,((6,7),)),
-        (1,1,((2,1),)),
-        (1,4,((5,4,4),(3,1,3))),
-        (1,5,((5,1,5),)),
+    ),
+    (
+        (1,4,((3,1,3),)),
         (1,6,((3,1),)),
-        (1,7,((5,1,4),)),
-    ),
-    (
+    ),
+    (
+        (1,1,((4,2,3),)),
+        (1,2,((2,3,4),(1,1,3))),
+        (1,3,((0,7,6),(5,7,4))),
+        (1,4,((1,6),)),
+        (1,6,((3,6,5),)),
         (0,0,((3,2,0,4,6),)),
         (0,2,((3,2),)),
         (0,6,((3,5),(1,6,1,0))),
-        (1,1,((4,2,3),)),
-        (1,2,((2,3,4),(1,1,3),(2,6))),
-        (1,3,((0,7,6),(5,7,4))),
-        (1,4,((1,6),)),
+    ),
+    (
+        (1,2,((2,6),)),
         (1,5,((1,0),)),
-        (1,6,((3,6,5),(4,6,4,3))),
-    ),
-    (
+        (1,6,((4,6,4,3),)),
+    ),
+    (
+        (1,1,((5,0),)),
+        (1,4,((2,5,3,4),)),
+        (1,5,((5,6,5,3),)),
+        (1,7,((1,0,3),(5,6,5))),
         (0,0,((6,5,0,3),(6,3,1,3,6))),
         (0,1,((7,3,1),(7,7))),
         (0,2,((5,7,2,0),(0,7))),
         (0,3,((2,2),(7,5))),
         (0,4,((2,1,1),(2,4,0))),
-        (0,5,((6,3),(1,3),(0,0))),
+        (0,5,((6,3),(1,3))),
         (0,6,((0,6),)),
-        (0,7,((2,2),(1,7,2,1))),
-        (1,1,((5,0),)),
-        (1,4,((2,5,3,4),(1,4))),
-        (1,5,((5,6,5,3),(2,2,4,3))),
-        (1,7,((1,0,3),(5,6,5),(7,1,3))),
-    ),
-    (
+        (0,7,((2,2),)),
+    ),
+    (
+        (1,4,((1,4),)),
+        (1,5,((2,2,4,3),)),
+        (1,7,((7,1,3),)),
+        (0,5,((0,0),)),
+        (0,7,((1,7,2,1),)),
+    ),
+    (
+        (1,2,((3,5),)),
+        (1,3,((1,6),)),
+        (1,6,((3,7,5),(1,6,3))),
         (0,0,((1,5,5),)),
         (0,3,((2,7,0),)),
         (0,6,((0,1,1,0),)),
+    ),
+    (
         (1,1,((6,1,3,5),)),
-        (1,2,((3,5),)),
-        (1,3,((1,6),(6,2,4,5))),
-        (1,6,((3,7,5),(1,6,3))),
-    ),
-    (
+        (1,3,((6,2,4,5),)),
+    ),
+    (
+        (1,2,((7,7,3),)),
+        (1,3,((3,7),)),
+        (1,4,((4,7),)),
+        (1,5,((4,1,4),)),
+        (1,7,((4,1),)),
         (0,0,((6,6,0,3),(4,3,4,6))),
-        (0,1,((0,2),(3,1),(6,0,0))),
-        (0,2,((3,0,2),(3,6),(6,5))),
-        (0,3,((5,1,1),(5,3,0))),
-        (0,4,((2,3,1),(1,1))),
+        (0,1,((0,2),(3,1))),
+        (0,2,((3,0,2),)),
+        (0,3,((5,1,1),)),
+        (0,4,((2,3,1),)),
         (0,5,((3,2),(1,4))),
         (0,6,((0,7,1),)),
-        (0,7,((1,3,0),(2,0))),
-        (1,2,((7,7,3),(1,2,4))),
-        (1,3,((3,7),)),
-        (1,4,((4,7),(6,0,3,4))),
-        (1,5,((4,1,4),(2,4,5,3),(7,4,4,3))),
-        (1,7,((4,1),(2,4,5))),
-    ),
-    (
+        (0,7,((1,3,0),)),
+    ),
+    (
+        (1,2,((1,2,4),)),
+        (1,4,((6,0,3,4),)),
+        (1,5,((2,4,5,3),(7,4,4,3))),
+        (1,7,((2,4,5),)),
+        (0,1,((6,0,0),)),
+        (0,2,((3,6),(6,5))),
+        (0,3,((5,3,0),)),
+        (0,4,((1,1),)),
+        (0,7,((2,0),)),
+    ),
+    (
+        (1,1,((7,1),)),
+        (1,6,((2,1,4,3),(1,4,4))),
         (0,3,((6,2),)),
+    ),
+    (
+        (1,1,((1,3,3,5),(3,7))),
+        (1,3,((4,7),(3,4,4,5))),
+        (1,6,((4,7,3),)),
         (0,6,((5,0),)),
-        (1,1,((7,1),(1,3,3,5),(3,7))),
-        (1,3,((4,7),(3,4,4,5))),
-        (1,6,((2,1,4,3),(1,4,4),(4,7,3))),
-    ),
-    (
+    ),
+    (
+        (1,4,((0,4,6),)),
+        (1,5,((3,0),)),
+        (1,7,((2,6,3,4),)),
+    ),
+    (
+        (1,2,((5,4,4),(3,3,3))),
+        (1,4,((4,2,3,4),)),
+        (1,5,((3,1),)),
+        (1,7,((4,4,3),(5,4,4))),
         (0,0,((7,0,5),(4,5,4,6))),
         (0,1,((7,5,2,1),(6,1))),
         (0,2,((4,0),(4,1,1))),
@@ -457,18 +613,28 @@
         (0,5,((6,5),(3,7,1))),
         (0,6,((5,6),)),
         (0,7,((2,6),)),
-        (1,2,((5,4,4),(3,3,3))),
-        (1,4,((0,4,6),(4,2,3,4))),
-        (1,5,((3,0),(3,1))),
-        (1,7,((2,6,3,4),(4,4,3),(5,4,4))),
     ),
     (
         (0,5,((7,4,1,0),)),
-        (0,6,((0,2,1,0),)),
+    ),
+    (
         (1,1,((2,3),)),
         (1,6,((2,3,4),)),
-    ),
-    (
+        (0,6,((0,2,1,0),)),
+    ),
+    (
+        (1,1,((6,5,3,5),)),
+        (1,3,((3,2,4,5),(1,1))),
+        (1,4,((1,0),)),
+        (1,6,((5,6,5),)),
+        (0,7,((2,1),)),
+    ),
+    (
+        (1,1,((5,1),)),
+        (1,2,((3,6,4,3),(5,7,5))),
+        (1,5,((4,6,5),(7,7,4,3))),
+        (1,6,((5,0,4,3),)),
+        (1,7,((4,6,3),)),
         (0,0,((5,2,0,3),(7,2,4))),
         (0,1,((7,6,1),)),
         (0,2,((3,5),)),
@@ -476,38 +642,41 @@
         (0,4,((7,6),)),
         (0,5,((6,6),(1,6))),
         (0,6,((1,5),)),
-        (0,7,((2,1),(1,4,0))),
-        (1,1,((6,5,3,5),(5,1))),
-        (1,2,((3,6,4,3),(5,7,5))),
-        (1,3,((3,2,4,5),(1,1))),
-        (1,4,((1,0),)),
-        (1,5,((4,6,5),(7,7,4,3))),
-        (1,6,((5,6,5),(5,0,4,3))),
-        (1,7,((4,6,3),)),
-    ),
-    (
+        (0,7,((1,4,0),)),
+    ),
+    (
+        (1,2,((4,2,5),)),
+        (1,3,((5,6),)),
+        (1,4,((6,4,3,4),)),
+        (1,5,((2,5,5),)),
+        (1,7,((2,5,5,4),)),
         (0,1,((3,2),(3,6))),
         (0,2,((4,4,1),)),
         (0,3,((5,5,0),)),
         (0,4,((2,5,0),)),
-        (1,2,((4,2,5),)),
-        (1,3,((5,6),)),
-        (1,4,((6,4,3,4),(2,2))),
-        (1,5,((2,5,5),)),
+    ),
+    (
+        (1,4,((2,2),)),
         (1,6,((5,1,5),)),
-        (1,7,((2,5,5,4),)),
-    ),
-    (
+    ),
+    (
+        (1,1,((6,3,3,5),)),
+        (1,3,((4,3,4,5),)),
+        (1,4,((7,1),)),
         (0,6,((0,3,1),)),
         (0,7,((0,3),(2,3))),
-        (1,1,((6,3,3,5),)),
+    ),
+    (
         (1,2,((3,7),)),
-        (1,3,((4,3,4,5),)),
-        (1,4,((7,1),)),
         (1,5,((2,1,4),)),
         (1,6,((2,2,5,3),(7,1,4))),
     ),
     (
+        (1,2,((6,2,4,5),(6,1,3))),
+        (1,3,((2,4),)),
+        (1,4,((1,5,3,4),)),
+        (1,5,((6,0,5),)),
+        (1,7,((6,2),(1,6),(6,0,5,4))),
         (0,0,((2,7,0,3,5,6),(6,7,4,5,6),(2,0,1,3,5,6))),
         (0,1,((4,2),(6,5))),
         (0,2,((4,6),(4,7))),
@@ -516,67 +685,99 @@
         (0,5,((0,4,0),(0,1))),
         (0,6,((1,7),)),
         (0,7,((0,0,0),)),
+    ),
+    (
         (1,1,((5,6),)),
-        (1,2,((6,2,4,5),(6,1,3))),
-        (1,3,((2,4),(7,7))),
-        (1,4,((1,5,3,4),)),
-        (1,5,((6,0,5),)),
-        (1,7,((6,2),(1,6),(6,0,5,4))),
-    ),
-    (
+        (1,3,((7,7),)),
+    ),
+    (
+        (1,6,((2,6),)),
         (0,6,((5,5,0),)),
+    ),
+    (
         (1,1,((6,6,3,5),(1,2,6))),
         (1,3,((4,5,4,5,6),)),
         (1,4,((4,1),(2,6,3))),
         (1,5,((3,3,4,3),)),
-        (1,6,((2,6),(2,4,5))),
-    ),
-    (
+        (1,6,((2,4,5),)),
+    ),
+    (
+        (1,2,((3,4,4,5,6),)),
+        (1,5,((1,4,5),)),
+        (1,7,((3,4,3,6),(2,1))),
         (0,0,((5,3,3,5,6),(7,3,4,5,6))),
-        (0,1,((0,6),(6,6))),
-        (0,2,((4,5,0),(5,2))),
-        (0,3,((6,0),(5,7))),
-        (0,4,((3,1),(1,2))),
+        (0,1,((0,6),)),
+        (0,2,((4,5,0),)),
+        (0,3,((6,0),)),
+        (0,4,((3,1),)),
         (0,5,((2,4),(0,7,1))),
+        (0,7,((1,6,0),)),
+    ),
+    (
+        (1,1,((2,4),)),
+        (1,2,((1,3,3,6),)),
+        (1,4,((7,0,3,4),(7,4))),
+        (1,5,((4,2),)),
+        (1,7,((4,2,5),)),
+        (0,1,((6,6),)),
+        (0,2,((5,2),)),
+        (0,3,((5,7),)),
+        (0,4,((1,2),)),
         (0,6,((7,4),)),
-        (0,7,((1,6,0),)),
-        (1,1,((2,4),)),
-        (1,2,((3,4,4,5,6),(1,3,3,6))),
-        (1,4,((7,0,3,4),(7,4))),
-        (1,5,((1,4,5),(4,2))),
-        (1,7,((3,4,3,6),(2,1),(4,2,5))),
-    ),
-    (
-        (0,6,((0,5,1,0),)),
+    ),
+    (
+        (1,3,((3,3,6),)),
+    ),
+    (
         (1,1,((5,2,3,5),(5,4))),
-        (1,3,((3,3,6),(7,2,4,5))),
+        (1,3,((7,2,4,5),)),
         (1,4,((4,4),)),
         (1,6,((5,4,4),)),
-    ),
-    (
+        (0,6,((0,5,1,0),)),
+    ),
+    (
+        (1,3,((2,5),)),
+        (1,5,((2,3),)),
+        (1,6,((7,4,3),)),
+        (0,5,((7,5,1),)),
+    ),
+    (
+        (1,2,((3,2,4,6),(6,5,3))),
+        (1,5,((6,1,3),(6,4,5))),
+        (1,7,((3,2,3,4),(4,7),(6,4,5))),
         (0,0,((5,5,3,5,6),(7,5,3,4,5))),
         (0,1,((4,1),(5,2))),
         (0,2,((7,1,0),(5,1))),
         (0,3,((6,4),)),
         (0,4,((3,5,1),(1,0))),
-        (0,5,((7,5,1),(0,6),(0,2,1))),
+        (0,5,((0,6),(0,2,1))),
         (0,7,((0,1,0),)),
-        (1,2,((3,2,4,6),(6,5,3))),
-        (1,3,((2,5),)),
-        (1,5,((2,3),(6,1,3),(6,4,5))),
-        (1,6,((7,4,3),)),
-        (1,7,((3,2,3,4),(4,7),(6,4,5))),
-    ),
-    (
-        (0,6,((0,4),(5,7))),
-        (0,7,((3,3),)),
+    ),
+    (
         (1,1,((4,6),)),
+        (1,6,((5,7,4,3),)),
+    ),
+    (
         (1,2,((5,6),)),
         (1,3,((3,6,6),)),
         (1,4,((7,7,4),)),
-        (1,6,((5,7,4,3),(2,5,5))),
-    ),
-    (
+        (1,6,((2,5,5),)),
+        (0,6,((0,4),(5,7))),
+        (0,7,((3,3),)),
+    ),
+    (
+        (1,1,((3,6),)),
+        (1,3,((6,7,4,5),(6,0))),
+        (1,4,((4,6),)),
+        (1,6,((7,7),)),
+    ),
+    (
+        (1,1,((2,7,3),)),
+        (1,2,((5,1,3),(4,3,4,6))),
+        (1,4,((2,7,3,4,6),)),
+        (1,5,((5,0),(1,3,4,3,6))),
+        (1,6,((4,2),)),
+        (1,7,((5,0,3),)),
         (0,0,((7,6,3,4,5,6),)),
         (0,1,((4,4),)),
         (0,2,((6,0),)),
@@ -584,148 +785,200 @@
         (0,4,((3,4,1),)),
         (0,5,((2,5),(0,3,1))),
         (0,7,((0,2),)),
-        (1,1,((3,6),(2,7,3))),
-        (1,2,((5,1,3),(4,3,4,6))),
-        (1,3,((6,7,4,5),(6,0))),
-        (1,4,((4,6),(2,7,3,4,6))),
-        (1,5,((5,0),(1,3,4,3,6))),
-        (1,6,((7,7),(4,2))),
-        (1,7,((5,0,3),)),
-    ),
-    (
+    ),
+    (
+        (1,1,((2,5,6),)),
+        (1,2,((6,3,3,5),)),
+        (1,5,((1,5,5,3),)),
+        (1,7,((1,5,5),(4,3,3,4,6))),
         (0,0,((1,7,3,4,5,6),)),
         (0,1,((2,7),)),
         (0,2,((5,4),)),
         (0,4,((1,3),)),
-        (1,1,((2,5,6),(2,0,3,6))),
-        (1,2,((6,3,3,5),(2,2))),
+    ),
+    (
+        (1,1,((2,0,3,6),)),
+        (1,2,((2,2),)),
         (1,4,((6,7,3),(2,1))),
-        (1,5,((1,5,5,3),)),
-        (1,7,((1,5,5),(4,3,3,4,6))),
-    ),
-    (
+    ),
+    (
+        (1,3,((7,3,4,5),(6,1))),
+        (1,4,((3,4,6),)),
+        (1,6,((6,0,5),)),
         (0,3,((4,5),)),
         (0,6,((3,0),)),
+    ),
+    (
         (1,1,((6,2),)),
-        (1,3,((7,3,4,5),(6,1),(4,2,6))),
-        (1,4,((3,4,6),)),
+        (1,3,((4,2,6),)),
         (1,5,((7,1),)),
-        (1,6,((6,0,5),(3,3,3))),
-    ),
-    (
+        (1,6,((3,3,3),)),
+    ),
+    (
+        (1,2,((4,5,4,6),(6,6,3))),
+        (1,5,((6,5,4,3),(2,6))),
+        (1,7,((2,2,5),(4,5,3,4,6))),
         (0,3,((2,0),)),
-        (0,4,((1,4),(3,7))),
+        (0,4,((1,4),)),
         (0,5,((2,7),(0,5))),
         (0,7,((5,5,0),)),
+    ),
+    (
         (1,1,((6,0,6),)),
-        (1,2,((4,5,4,6),(6,6,3))),
         (1,4,((2,0,3,4,6),)),
-        (1,5,((6,5,4,3),(2,6))),
-        (1,7,((2,2,5),(4,5,3,4,6),(7,0,5,4))),
-    ),
-    (
+        (1,7,((7,0,5,4),)),
+        (0,4,((3,7),)),
+    ),
+    (
+        (1,4,((3,3),)),
+        (1,6,((3,2,4,6),)),
+        (0,7,((3,5),)),
+    ),
+    (
+        (1,1,((5,3,3,5,6),(3,4,6))),
+        (1,3,((7,5),(1,3,6))),
+        (1,4,((3,2,6),)),
+        (1,6,((6,2,4),(6,1,3))),
         (0,3,((7,1),)),
         (0,4,((7,4),)),
-        (0,7,((3,5),(5,4))),
-        (1,1,((5,3,3,5,6),(3,4,6))),
-        (1,3,((7,5),(1,3,6))),
-        (1,4,((3,3),(3,2,6))),
-        (1,6,((3,2,4,6),(6,2,4),(6,1,3))),
-    ),
-    (
+        (0,7,((5,4),)),
+    ),
+    (
+        (1,2,((7,2,4),)),
+        (1,3,((6,4,4),)),
+        (1,5,((5,4),(6,3,4))),
+        (1,7,((7,4,5),)),
+        (0,7,((0,5,0),)),
+    ),
+    (
+        (1,1,((1,4),)),
+        (1,2,((5,2,3,5),)),
+        (1,5,((7,0,5),)),
+        (1,7,((7,2,3,4),)),
         (0,4,((0,0),)),
-        (0,7,((0,5,0),)),
-        (1,1,((1,4),)),
-        (1,2,((7,2,4),(5,2,3,5))),
-        (1,3,((6,4,4),)),
-        (1,5,((5,4),(6,3,4),(7,0,5))),
-        (1,7,((7,4,5),(7,2,3,4))),
-    ),
-    (
-        (0,7,((3,4),)),
+    ),
+    (
         (1,2,((2,4),)),
+        (1,7,((7,7),)),
+    ),
+    (
         (1,3,((7,6,4,5),(6,5))),
         (1,4,((1,3,4,6),)),
         (1,6,((3,4,4,6),)),
-        (1,7,((7,7),)),
-    ),
-    (
+        (0,7,((3,4),)),
+    ),
+    (
+        (1,1,((3,2,6),(5,5,3))),
+        (1,3,((1,5),)),
+        (1,4,((5,3,4),)),
+        (1,6,((1,3,6),(4,3,4,6))),
+    ),
+    (
+        (1,2,((6,7,4),)),
+        (1,4,((5,0),)),
+        (1,5,((5,7,5),(6,6,4,3),(6,7,6))),
+        (1,7,((5,7,3),(6,7,4))),
         (0,4,((0,7),(1,6))),
-        (1,1,((3,2,6),(5,5,3))),
-        (1,2,((6,7,4),)),
-        (1,3,((1,5),)),
-        (1,4,((5,3,4),(5,0))),
-        (1,5,((5,7,5),(6,6,4,3),(6,7,6))),
-        (1,6,((1,3,6),(4,3,4,6))),
-        (1,7,((5,7,3),(6,7,4))),
-    ),
-    (
-        (1,1,((6,4),(7,5,3))),
+    ),
+    (
+        (1,1,((6,4),)),
+        (1,4,((7,3,3),)),
+    ),
+    (
+        (1,1,((7,5,3),)),
         (1,2,((2,5),)),
-        (1,4,((7,3,3),(4,3,6),(6,5))),
-    ),
-    (
+        (1,4,((4,3,6),(6,5))),
+    ),
+    (
+        (1,1,((4,3,6),)),
+        (1,2,((2,7,3,6),(2,0,5,6))),
+        (1,3,((1,7,4,5,6),(5,1))),
+        (1,6,((6,3,3,6),(1,5,5))),
+    ),
+    (
+        (1,2,((7,3,4),)),
+        (1,3,((2,2),)),
+        (1,5,((5,2,4),)),
+        (1,6,((4,5,6),)),
+        (1,7,((2,7,6),(2,0,5,6))),
         (0,4,((7,5),)),
-        (1,1,((4,3,6),)),
-        (1,2,((2,7,3,6),(2,0,5,6),(7,3,4))),
-        (1,3,((1,7,4,5,6),(5,1),(2,2))),
-        (1,5,((5,2,4),)),
-        (1,6,((6,3,3,6),(1,5,5),(4,5,6))),
-        (1,7,((2,7,6),(2,0,5,6))),
-    ),
-    (
+    ),
+    (
+        (1,1,((1,5),)),
+        (1,7,((3,3,6),(7,3,6))),
         (0,4,((0,1),)),
-        (1,1,((1,5),)),
+    ),
+    (
         (1,2,((6,0,6),)),
         (1,5,((3,2,6),)),
-        (1,7,((3,3,6),(7,3,6))),
-    ),
-    (
-        (1,1,((7,6,5,6),(4,5,5,6))),
-        (1,3,((6,3,6),(7,0,6))),
-        (1,4,((6,3),(4,5,6),(5,5,3,4))),
-        (1,5,((2,7,3,6),(2,0,6),(6,2,4,6))),
+    ),
+    (
+        (1,1,((7,6,5,6),)),
+        (1,3,((6,3,6),)),
+        (1,4,((6,3),)),
+        (1,5,((2,7,3,6),(2,0,6))),
+    ),
+    (
+        (1,1,((4,5,5,6),)),
+        (1,3,((7,0,6),)),
+        (1,4,((4,5,6),(5,5,3,4))),
+        (1,5,((6,2,4,6),)),
         (1,6,((7,0,5),(6,5,3))),
     ),
     (
-        (0,4,((0,2),(5,5))),
-        (1,1,((7,0),)),
-        (1,2,((6,4,5,6),(5,3,6))),
-        (1,4,((7,5,3,4),)),
+        (1,2,((6,4,5,6),)),
         (1,5,((5,3,3,6),)),
         (1,6,((5,2),)),
-        (1,7,((6,1,3),(7,6,4))),
+        (1,7,((6,1,3),)),
+        (0,4,((0,2),(5,5))),
+    ),
+    (
+        (1,1,((7,0),)),
+        (1,2,((5,3,6),)),
+        (1,4,((7,5,3,4),)),
+        (1,7,((7,6,4),)),
+    ),
+    (
+        (1,7,((1,3,6),)),
     ),
     (
         (1,1,((1,7,5,6),(7,2))),
         (1,3,((6,6,6),)),
         (1,4,((7,2,6),(6,6,6))),
-        (1,7,((1,3,6),)),
-    ),
-    (
-        (0,4,((0,3),(0,5))),
+    ),
+    (
+        (1,3,((7,4,6),)),
+        (1,6,((6,6,3),(7,2,4))),
+        (0,4,((0,3),)),
+    ),
+    (
         (1,1,((5,7,6),)),
         (1,2,((7,6),)),
-        (1,3,((7,4,6),)),
         (1,5,((7,3,3),(3,4,6))),
-        (1,6,((6,6,3),(7,2,4))),
         (1,7,((6,3,6),)),
+        (0,4,((0,5),)),
+    ),
+    (
+        (1,6,((2,0,6),)),
+        (1,7,((1,7,4,6),(5,3,5))),
     ),
     (
         (1,2,((1,5),(5,5,3,5,6))),
         (1,3,((5,2,5),)),
         (1,4,((7,6,6),)),
-        (1,6,((2,0,6),)),
-        (1,7,((1,7,4,6),(5,3,5))),
     ),
     (
         (1,1,((6,7,6),)),
-        (1,2,((7,5,5,6),(1,7,6))),
+        (1,2,((7,5,5,6),)),
         (1,3,((2,0,6),)),
         (1,4,((5,7,6),(5,2,6))),
+        (1,6,((6,7),)),
+    ),
+    (
+        (1,2,((1,7,6),)),
         (1,5,((4,3,6),)),
-        (1,6,((6,7),)),
-    ),
+    ),
+    (),
     (
         (1,2,((7,0,6),)),
         (1,4,((1,7,6),)),
@@ -734,30 +987,43 @@
     (
         (1,1,((7,3,6),)),
         (1,3,((2,7,6),)),
-        (1,4,((6,1),(6,2,6))),
-        (1,5,((7,6),(4,5,6),(5,5,6),(7,5,6))),
+        (1,4,((6,1),)),
+        (1,5,((7,6),(4,5,6))),
+    ),
+    (
+        (1,4,((6,2,6),)),
+        (1,5,((5,5,6),(7,5,6))),
         (1,6,((6,4,6),)),
         (1,7,((5,5,6),)),
     ),
     (
+        (1,6,((7,6),)),
+        (1,7,((7,5,6),)),
+    ),
+    (
         (1,5,((7,2,6),)),
-        (1,6,((7,6),(2,7,6),(5,3,6))),
-        (1,7,((7,5,6),)),
+        (1,6,((2,7,6),(5,3,6))),
     ),
     (
         (1,7,((6,6,6),)),
     ),
+    (),
     (
         (1,3,((5,3,6),)),
+        (1,6,((1,7,6),)),
+    ),
+    (
         (1,5,((1,7,6),)),
-        (1,6,((1,7,6),(7,5,6))),
+        (1,6,((7,5,6),)),
         (1,7,((5,2,6),)),
     ),
+    (),
     (),
     (
         (1,3,((5,5,6),)),
         (1,6,((7,3,6),)),
     ),
+    (),
     (
         (1,6,((5,5,6),)),
     ),

time: 72 us -> 71 us (0.986)
  the two profiles are of different devices: /device:TPU:35 before, /device:TPU:7 now
where the time goes in v4:
time: 71 us; the launch traced here: 70.7 us
  Pallas kernels  70.6 us (99%)
    pallas_call x1, Pallas kernels, gather(): pl.pallas_call(gather_kernel, out_shape=(pltpu.VMEM((8 * reads, bins), we...  56 us
    pallas_call x1, Pallas kernels, product(): pl.pallas_call(kernel, out_shape=jax.ShapeDtypeStruct((rows, cols), left....  14.6 us

profile of v4, /device:TPU:7, one launch (start us, length us, event | category | flops | bytes accessed | tf_op | source)
XLA Modules:
  0.0 70.7 jit_solution(16405206313981849664)
XLA Ops:
  0.0 56.0 %gather.1 = (bf16[2048,1024]{1,0:T(8,128)(2,1)S(1)}, bf16[4096,1024]{1,0:T(8,128)(2,1)S(1)}) custom-call(s32[1,2]{1,0:T(1,128)} %pattern_hbm.1, bf16[256,1024]{1,0:T(8,128)(2,1)} %weights_hbm.1), custom_call_target="tpu_custom_call" | custom-call | tf_op jit(solution)/shard_map/gather/pallas_call | solution.py:1200
  56.0 14.6 %product.1 = bf16[2048,4096]{1,0:T(8,128)(2,1)} custom-call(bf16[2048,1024]{1,0:T(8,128)(2,1)S(1)} %get-tuple-element.7.refs_0_, bf16[4096,1024]{1,0:T(8,128)(2,1)S(1)} %get-tuple-element.8.refs_1_), custom_call_target="tpu_custom_call" | custom-call | tf_op jit(solution)/shard_map/product/pallas_call | solution.py:1287

commit v5 on v4

--- a/solution.py
+++ b/solution.py
@@ -9,10 +9,10 @@
 
 MESH = pl.DeviceIdType.MESH
 CHUNKS = 8
-UNITS = 2
+UNITS = 4
 SLOTS = (
     (
-        (0,0,((0,0,1,5),(0,1,0,1,4),(0,2,1,4),(0,3,0,3,6),(0,4,0,1,4),(0,5,0,3),(0,6,1,5),(0,7,0,1,5,6))),
+        (0,0,((0,0,1,5),(0,1,0,1,4,6),(0,2,1,4),(0,3,0,3,6),(0,4,0,1,4),(0,5,0,3,6),(0,6,1,5),(0,7,0,1,5,6))),
         (0,1,((1,0,0,1),(1,1,0,1,2),(1,2,0,1,2),(1,3,0),(1,4,0,1),(1,5,0,2),(1,6,0,1),(1,7,0,2))),
         (0,2,((2,0,1,2),(2,1,0,2),(2,2,1),(2,3,0,1,2),(2,4,0,2),(2,5,0,1,2),(2,6,1),(2,7,2))),
         (0,3,((3,0,0,2),(3,1,0,1,2),(3,2,2),(3,3,1),(3,4,1),(3,5,0),(3,6,0,2),(3,7,0,1,2))),
@@ -62,7 +62,7 @@
     ),
     (
         (1,4,((0,6,3,4),)),
-        (0,0,((3,1,4),(1,1,5))),
+        (0,0,((3,1,4,6),(1,1,5,6))),
         (0,1,((2,2,1,2),)),
         (0,2,((1,1,0),)),
         (0,3,((0,1,1),)),
@@ -84,7 +84,7 @@
     (),
     (
         (1,1,((0,5,3,5),)),
-        (0,0,((4,1,1,3),)),
+        (0,0,((4,1,1,3,6),)),
         (0,1,((5,3,0),)),
         (0,2,((6,2,1),)),
         (0,5,((1,2,0),)),
@@ -95,7 +95,7 @@
         (0,3,((7,4,0,1),)),
     ),
     (
-        (1,4,((0,7,3,4),)),
+        (1,4,((0,7,3,4,6),)),
         (0,0,((3,5,0,5),(1,2,1,5))),
         (0,1,((2,3),(0,4))),
         (0,2,((1,2),(3,4,1,2))),
@@ -160,13 +160,13 @@
         (0,7,((3,6,0,1),)),
     ),
     (
-        (1,2,((0,2,4),)),
+        (1,2,((0,2,4,6),)),
         (0,3,((4,2,0,1),)),
     ),
     (
         (1,2,((0,5,3),)),
         (1,4,((1,1,3,4),)),
-        (0,0,((3,7,5),(1,6,3))),
+        (0,0,((3,7,5,6),(1,6,3))),
         (0,1,((2,6,1,2),(0,7))),
         (0,2,((1,4,2),(0,0,1,2))),
         (0,3,((0,6,1,2),(6,1,0))),
@@ -176,22 +176,22 @@
         (0,7,((6,6,0),)),
     ),
     (
-        (1,3,((3,1,4,5),)),
+        (1,3,((3,1,4,5,6),)),
         (0,5,((2,0,1),)),
         (0,6,((1,1,0),)),
         (0,7,((4,6,1,2),)),
     ),
     (
-        (0,0,((4,7,0,1,3),)),
+        (0,0,((4,7,0,1,3,6),)),
         (0,1,((5,7,0,1),)),
         (0,6,((2,5,0),)),
         (0,7,((3,7,1),)),
     ),
     (
-        (1,1,((4,1,3),)),
-        (1,2,((0,4,4,5),)),
-        (1,5,((0,7,5,3),)),
-        (1,7,((0,7),)),
+        (1,1,((4,1,3,6),)),
+        (1,2,((0,4,4,5,6),)),
+        (1,5,((0,7,5,3,6),)),
+        (1,7,((0,7,6),)),
         (0,2,((6,6,0),)),
         (0,3,((4,3,1),)),
         (0,5,((2,2,0,1),)),
@@ -220,7 +220,7 @@
     ),
     (
         (1,1,((0,1),)),
-        (1,6,((0,1,4,3),)),
+        (1,6,((0,1,4,3,6),)),
     ),
     (
         (1,1,((4,4,3,5),)),
@@ -232,14 +232,14 @@
     ),
     (
         (1,2,((3,0,4),)),
-        (1,3,((0,3),)),
+        (1,3,((0,3,6),)),
         (1,5,((4,0),)),
         (1,7,((4,0,4),)),
     ),
     (
         (1,2,((4,0,3),)),
         (1,4,((1,2,3,4),)),
-        (0,0,((2,3,4,5),(2,2,1,3))),
+        (0,0,((2,3,4,5),(2,2,1,3,6))),
         (0,1,((6,2,1),(3,5,0,2))),
         (0,2,((1,6,0,2),(0,1,2))),
         (0,3,((1,0),(1,3,0))),
@@ -257,16 +257,16 @@
     (
         (1,5,((0,5,4,3),)),
         (1,7,((0,2,3,4),)),
-        (0,0,((5,1,0,1,5),)),
+        (0,0,((5,1,0,1,5,6),)),
         (0,1,((6,4,1),)),
         (0,3,((6,5,1,0),)),
         (0,6,((1,0,1,0),)),
         (0,7,((0,4,0),)),
     ),
     (
-        (1,1,((0,0,3),(0,2,6),(1,6,3,5))),
-        (1,2,((3,1,4),)),
-        (1,3,((4,6,4),(0,5))),
+        (1,1,((0,0,3,6),(0,2,6),(1,6,3,5))),
+        (1,2,((3,1,4,6),)),
+        (1,3,((4,6,4),(0,5,6))),
         (1,5,((1,1,5),)),
         (1,7,((1,1,4),)),
         (0,2,((7,0,0,1),)),
@@ -295,21 +295,21 @@
         (0,5,((2,6,0,1),(7,6,1))),
     ),
     (
-        (1,1,((0,4),(4,7,3,5))),
-        (1,2,((4,1,3,5),)),
+        (1,1,((0,4,6),(4,7,3,5))),
+        (1,2,((4,1,3,5,6),)),
         (1,3,((2,1,4),(0,6))),
-        (1,6,((0,7,5),)),
+        (1,6,((0,7,5,6),)),
         (1,7,((0,0),)),
         (0,6,((3,1,1),)),
     ),
     (
         (1,3,((1,0),)),
-        (1,5,((3,5,5),(0,1))),
+        (1,5,((3,5,5),(0,1,6))),
         (1,7,((3,5,5,4),)),
     ),
     (
         (1,2,((1,4),)),
-        (1,4,((3,7,3,4),)),
+        (1,4,((3,7,3,4,6),)),
         (0,0,((2,4,0,5),(2,6,1,3,4))),
         (0,1,((6,3,1),(4,7))),
         (0,2,((5,0,2),(7,3,0,1),(0,2,1,2))),
@@ -336,10 +336,10 @@
         (1,1,((2,2,5),(3,0))),
         (1,3,((5,0,4),(4,0))),
         (1,5,((1,2,3),)),
-        (1,7,((0,1,3),(1,2,5))),
-    ),
-    (
-        (0,0,((7,7,0,3),(5,7,4))),
+        (1,7,((0,1,3,6),(1,2,5))),
+    ),
+    (
+        (0,0,((7,7,0,3),(5,7,4,6))),
         (0,1,((3,7),)),
         (0,2,((0,3,0,2),)),
         (0,3,((1,2),)),
@@ -363,7 +363,7 @@
         (1,6,((0,5,3),(0,2,6))),
     ),
     (
-        (1,1,((3,1),(7,4,3,5))),
+        (1,1,((3,1,6),(7,4,3,5))),
         (1,2,((0,0,3,6),)),
         (1,3,((7,1,4,5),)),
         (1,5,((4,4,3),)),
@@ -378,9 +378,9 @@
     ),
     (
         (1,1,((0,7),)),
-        (1,3,((4,1),)),
+        (1,3,((4,1,6),)),
         (1,4,((5,1,3,4),)),
-        (0,0,((2,5,5),(3,3,3),(6,0,1,0,5))),
+        (0,0,((2,5,5,6),(3,3,3),(6,0,1,0,5))),
         (0,1,((0,0,2),(5,1))),
         (0,2,((5,3,0),(0,4))),
         (0,3,((4,4,1),(1,6))),
@@ -397,7 +397,7 @@
     (
         (1,2,((1,6,3),)),
         (1,6,((1,1,5),)),
-        (1,7,((3,1,3,4),)),
+        (1,7,((3,1,3,4,6),)),
         (0,5,((3,5,1,0),)),
         (0,6,((1,3,1,0),)),
     ),
@@ -409,8 +409,8 @@
     ),
     (
         (1,3,((3,5,4),)),
-        (1,5,((3,7,5),)),
-        (1,6,((1,0,4,3),)),
+        (1,5,((3,7,5,6),)),
+        (1,6,((1,0,4,3,6),)),
         (0,0,((4,2,3,5),(6,2,4))),
         (0,1,((7,2,1),)),
         (0,2,((5,5,2,0),)),
@@ -421,10 +421,10 @@
         (0,7,((2,7,2,0),)),
     ),
     (
-        (1,1,((1,1),)),
+        (1,1,((1,1,6),)),
         (1,3,((4,4),)),
         (1,4,((5,6,3,4),)),
-        (1,7,((3,7,5,4),)),
+        (1,7,((3,7,5,4,6),)),
         (0,1,((7,4,2),)),
         (0,2,((4,2,1),)),
         (0,3,((7,0,0),)),
@@ -439,7 +439,7 @@
     ),
     (
         (1,1,((7,7,3,5),)),
-        (1,2,((4,7,3),)),
+        (1,2,((4,7,3,6),)),
         (1,3,((2,6,5),)),
         (1,6,((1,2,5),)),
         (1,7,((1,4,3,4),)),
@@ -453,7 +453,7 @@
         (1,4,((2,4,3,4),)),
         (1,5,((4,7,4,3),(0,2,6))),
         (1,7,((2,3,4),)),
-        (0,0,((6,1,0,3),(6,4,1,5))),
+        (0,0,((6,1,0,3,6),(6,4,1,5))),
         (0,1,((6,7,1),(2,4))),
         (0,2,((0,5,0,2),(0,6,1))),
         (0,3,((4,7,1),(7,3))),
@@ -464,8 +464,8 @@
     ),
     (
         (1,2,((7,1,4,5),)),
-        (1,4,((0,1),)),
-        (1,6,((4,1,4,3),)),
+        (1,4,((0,1,6),)),
+        (1,6,((4,1,4,3,6),)),
         (0,1,((7,1,0),)),
         (0,3,((5,2,1,0),)),
         (0,7,((6,4),)),
@@ -507,12 +507,12 @@
         (0,7,((6,7),)),
     ),
     (
-        (1,4,((3,1,3),)),
-        (1,6,((3,1),)),
+        (1,4,((3,1,3,6),)),
+        (1,6,((3,1,6),)),
     ),
     (
         (1,1,((4,2,3),)),
-        (1,2,((2,3,4),(1,1,3))),
+        (1,2,((2,3,4),(1,1,3,6))),
         (1,3,((0,7,6),(5,7,4))),
         (1,4,((1,6),)),
         (1,6,((3,6,5),)),
@@ -522,15 +522,15 @@
     ),
     (
         (1,2,((2,6),)),
-        (1,5,((1,0),)),
+        (1,5,((1,0,6),)),
         (1,6,((4,6,4,3),)),
     ),
     (
         (1,1,((5,0),)),
-        (1,4,((2,5,3,4),)),
+        (1,4,((2,5,3,4,6),)),
         (1,5,((5,6,5,3),)),
-        (1,7,((1,0,3),(5,6,5))),
-        (0,0,((6,5,0,3),(6,3,1,3,6))),
+        (1,7,((1,0,3,6),(5,6,5))),
+        (0,0,((6,5,0,3,6),(6,3,1,3,6))),
         (0,1,((7,3,1),(7,7))),
         (0,2,((5,7,2,0),(0,7))),
         (0,3,((2,2),(7,5))),
@@ -549,8 +549,8 @@
     (
         (1,2,((3,5),)),
         (1,3,((1,6),)),
-        (1,6,((3,7,5),(1,6,3))),
-        (0,0,((1,5,5),)),
+        (1,6,((3,7,5,6),(1,6,3))),
+        (0,0,((1,5,5,6),)),
         (0,3,((2,7,0),)),
         (0,6,((0,1,1,0),)),
     ),
@@ -562,8 +562,8 @@
         (1,2,((7,7,3),)),
         (1,3,((3,7),)),
         (1,4,((4,7),)),
-        (1,5,((4,1,4),)),
-        (1,7,((4,1),)),
+        (1,5,((4,1,4,6),)),
+        (1,7,((4,1,6),)),
         (0,0,((6,6,0,3),(4,3,4,6))),
         (0,1,((0,2),(3,1))),
         (0,2,((3,0,2),)),
@@ -591,8 +591,8 @@
     ),
     (
         (1,1,((1,3,3,5),(3,7))),
-        (1,3,((4,7),(3,4,4,5))),
-        (1,6,((4,7,3),)),
+        (1,3,((4,7,6),(3,4,4,5,6))),
+        (1,6,((4,7,3,6),)),
         (0,6,((5,0),)),
     ),
     (
@@ -603,9 +603,9 @@
     (
         (1,2,((5,4,4),(3,3,3))),
         (1,4,((4,2,3,4),)),
-        (1,5,((3,1),)),
+        (1,5,((3,1,6),)),
         (1,7,((4,4,3),(5,4,4))),
-        (0,0,((7,0,5),(4,5,4,6))),
+        (0,0,((7,0,5,6),(4,5,4,6))),
         (0,1,((7,5,2,1),(6,1))),
         (0,2,((4,0),(4,1,1))),
         (0,3,((5,6),(7,6))),
@@ -618,21 +618,21 @@
         (0,5,((7,4,1,0),)),
     ),
     (
-        (1,1,((2,3),)),
+        (1,1,((2,3,6),)),
         (1,6,((2,3,4),)),
         (0,6,((0,2,1,0),)),
     ),
     (
         (1,1,((6,5,3,5),)),
-        (1,3,((3,2,4,5),(1,1))),
-        (1,4,((1,0),)),
+        (1,3,((3,2,4,5),(1,1,6))),
+        (1,4,((1,0,6),)),
         (1,6,((5,6,5),)),
         (0,7,((2,1),)),
     ),
     (
-        (1,1,((5,1),)),
+        (1,1,((5,1,6),)),
         (1,2,((3,6,4,3),(5,7,5))),
-        (1,5,((4,6,5),(7,7,4,3))),
+        (1,5,((4,6,5,6),(7,7,4,3))),
         (1,6,((5,0,4,3),)),
         (1,7,((4,6,3),)),
         (0,0,((5,2,0,3),(7,2,4))),
@@ -646,18 +646,18 @@
     ),
     (
         (1,2,((4,2,5),)),
-        (1,3,((5,6),)),
+        (1,3,((5,6,6),)),
         (1,4,((6,4,3,4),)),
-        (1,5,((2,5,5),)),
-        (1,7,((2,5,5,4),)),
+        (1,5,((2,5,5,6),)),
+        (1,7,((2,5,5,4,6),)),
         (0,1,((3,2),(3,6))),
         (0,2,((4,4,1),)),
         (0,3,((5,5,0),)),
         (0,4,((2,5,0),)),
     ),
     (
-        (1,4,((2,2),)),
-        (1,6,((5,1,5),)),
+        (1,4,((2,2,6),)),
+        (1,6,((5,1,5,6),)),
     ),
     (
         (1,1,((6,3,3,5),)),
@@ -667,14 +667,14 @@
         (0,7,((0,3),(2,3))),
     ),
     (
-        (1,2,((3,7),)),
+        (1,2,((3,7,6),)),
         (1,5,((2,1,4),)),
-        (1,6,((2,2,5,3),(7,1,4))),
+        (1,6,((2,2,5,3,6),(7,1,4))),
     ),
     (
         (1,2,((6,2,4,5),(6,1,3))),
         (1,3,((2,4),)),
-        (1,4,((1,5,3,4),)),
+        (1,4,((1,5,3,4,6),)),
         (1,5,((6,0,5),)),
         (1,7,((6,2),(1,6),(6,0,5,4))),
         (0,0,((2,7,0,3,5,6),(6,7,4,5,6),(2,0,1,3,5,6))),
@@ -697,7 +697,7 @@
     (
         (1,1,((6,6,3,5),(1,2,6))),
         (1,3,((4,5,4,5,6),)),
-        (1,4,((4,1),(2,6,3))),
+        (1,4,((4,1,6),(2,6,3))),
         (1,5,((3,3,4,3),)),
         (1,6,((2,4,5),)),
     ),
@@ -716,7 +716,7 @@
     (
         (1,1,((2,4),)),
         (1,2,((1,3,3,6),)),
-        (1,4,((7,0,3,4),(7,4))),
+        (1,4,((7,0,3,4,6),(7,4))),
         (1,5,((4,2),)),
         (1,7,((4,2,5),)),
         (0,1,((6,6),)),
@@ -736,16 +736,16 @@
         (0,6,((0,5,1,0),)),
     ),
     (
-        (1,3,((2,5),)),
-        (1,5,((2,3),)),
+        (1,3,((2,5,6),)),
+        (1,5,((2,3,6),)),
         (1,6,((7,4,3),)),
         (0,5,((7,5,1),)),
     ),
     (
         (1,2,((3,2,4,6),(6,5,3))),
-        (1,5,((6,1,3),(6,4,5))),
-        (1,7,((3,2,3,4),(4,7),(6,4,5))),
-        (0,0,((5,5,3,5,6),(7,5,3,4,5))),
+        (1,5,((6,1,3,6),(6,4,5))),
+        (1,7,((3,2,3,4),(4,7,6),(6,4,5))),
+        (0,0,((5,5,3,5,6),(7,5,3,4,5,6))),
         (0,1,((4,1),(5,2))),
         (0,2,((7,1,0),(5,1))),
         (0,3,((6,4),)),
@@ -754,30 +754,30 @@
         (0,7,((0,1,0),)),
     ),
     (
-        (1,1,((4,6),)),
-        (1,6,((5,7,4,3),)),
-    ),
-    (
-        (1,2,((5,6),)),
+        (1,1,((4,6,6),)),
+        (1,6,((5,7,4,3,6),)),
+    ),
+    (
+        (1,2,((5,6,6),)),
         (1,3,((3,6,6),)),
         (1,4,((7,7,4),)),
-        (1,6,((2,5,5),)),
+        (1,6,((2,5,5,6),)),
         (0,6,((0,4),(5,7))),
         (0,7,((3,3),)),
     ),
     (
-        (1,1,((3,6),)),
+        (1,1,((3,6,6),)),
         (1,3,((6,7,4,5),(6,0))),
-        (1,4,((4,6),)),
+        (1,4,((4,6,6),)),
         (1,6,((7,7),)),
     ),
     (
-        (1,1,((2,7,3),)),
-        (1,2,((5,1,3),(4,3,4,6))),
+        (1,1,((2,7,3,6),)),
+        (1,2,((5,1,3,6),(4,3,4,6))),
         (1,4,((2,7,3,4,6),)),
-        (1,5,((5,0),(1,3,4,3,6))),
+        (1,5,((5,0,6),(1,3,4,3,6))),
         (1,6,((4,2),)),
-        (1,7,((5,0,3),)),
+        (1,7,((5,0,3,6),)),
         (0,0,((7,6,3,4,5,6),)),
         (0,1,((4,4),)),
         (0,2,((6,0),)),
@@ -788,9 +788,9 @@
     ),
     (
         (1,1,((2,5,6),)),
-        (1,2,((6,3,3,5),)),
-        (1,5,((1,5,5,3),)),
-        (1,7,((1,5,5),(4,3,3,4,6))),
+        (1,2,((6,3,3,5,6),)),
+        (1,5,((1,5,5,3,6),)),
+        (1,7,((1,5,5,6),(4,3,3,4,6))),
         (0,0,((1,7,3,4,5,6),)),
         (0,1,((2,7),)),
         (0,2,((5,4),)),
@@ -798,26 +798,26 @@
     ),
     (
         (1,1,((2,0,3,6),)),
-        (1,2,((2,2),)),
+        (1,2,((2,2,6),)),
         (1,4,((6,7,3),(2,1))),
     ),
     (
-        (1,3,((7,3,4,5),(6,1))),
+        (1,3,((7,3,4,5,6),(6,1,6))),
         (1,4,((3,4,6),)),
         (1,6,((6,0,5),)),
         (0,3,((4,5),)),
         (0,6,((3,0),)),
     ),
     (
-        (1,1,((6,2),)),
+        (1,1,((6,2,6),)),
         (1,3,((4,2,6),)),
         (1,5,((7,1),)),
         (1,6,((3,3,3),)),
     ),
     (
         (1,2,((4,5,4,6),(6,6,3))),
-        (1,5,((6,5,4,3),(2,6))),
-        (1,7,((2,2,5),(4,5,3,4,6))),
+        (1,5,((6,5,4,3,6),(2,6))),
+        (1,7,((2,2,5,6),(4,5,3,4,6))),
         (0,3,((2,0),)),
         (0,4,((1,4),)),
         (0,5,((2,7),(0,5))),
@@ -826,7 +826,7 @@
     (
         (1,1,((6,0,6),)),
         (1,4,((2,0,3,4,6),)),
-        (1,7,((7,0,5,4),)),
+        (1,7,((7,0,5,4,6),)),
         (0,4,((3,7),)),
     ),
     (
@@ -838,7 +838,7 @@
         (1,1,((5,3,3,5,6),(3,4,6))),
         (1,3,((7,5),(1,3,6))),
         (1,4,((3,2,6),)),
-        (1,6,((6,2,4),(6,1,3))),
+        (1,6,((6,2,4),(6,1,3,6))),
         (0,3,((7,1),)),
         (0,4,((7,4),)),
         (0,7,((5,4),)),
@@ -853,7 +853,7 @@
     (
         (1,1,((1,4),)),
         (1,2,((5,2,3,5),)),
-        (1,5,((7,0,5),)),
+        (1,5,((7,0,5,6),)),
         (1,7,((7,2,3,4),)),
         (0,4,((0,0),)),
     ),
@@ -862,49 +862,49 @@
         (1,7,((7,7),)),
     ),
     (
-        (1,3,((7,6,4,5),(6,5))),
+        (1,3,((7,6,4,5,6),(6,5,6))),
         (1,4,((1,3,4,6),)),
         (1,6,((3,4,4,6),)),
         (0,7,((3,4),)),
     ),
     (
-        (1,1,((3,2,6),(5,5,3))),
-        (1,3,((1,5),)),
+        (1,1,((3,2,6),(5,5,3,6))),
+        (1,3,((1,5,6),)),
         (1,4,((5,3,4),)),
         (1,6,((1,3,6),(4,3,4,6))),
     ),
     (
-        (1,2,((6,7,4),)),
-        (1,4,((5,0),)),
-        (1,5,((5,7,5),(6,6,4,3),(6,7,6))),
-        (1,7,((5,7,3),(6,7,4))),
+        (1,2,((6,7,4,6),)),
+        (1,4,((5,0,6),)),
+        (1,5,((5,7,5,6),(6,6,4,3),(6,7,6))),
+        (1,7,((5,7,3,6),(6,7,4))),
         (0,4,((0,7),(1,6))),
     ),
     (
-        (1,1,((6,4),)),
+        (1,1,((6,4,6),)),
         (1,4,((7,3,3),)),
     ),
     (
-        (1,1,((7,5,3),)),
-        (1,2,((2,5),)),
-        (1,4,((4,3,6),(6,5))),
+        (1,1,((7,5,3,6),)),
+        (1,2,((2,5,6),)),
+        (1,4,((4,3,6),(6,5,6))),
     ),
     (
         (1,1,((4,3,6),)),
         (1,2,((2,7,3,6),(2,0,5,6))),
-        (1,3,((1,7,4,5,6),(5,1))),
-        (1,6,((6,3,3,6),(1,5,5))),
-    ),
-    (
-        (1,2,((7,3,4),)),
-        (1,3,((2,2),)),
+        (1,3,((1,7,4,5,6),(5,1,6))),
+        (1,6,((6,3,3,6),(1,5,5,6))),
+    ),
+    (
+        (1,2,((7,3,4,6),)),
+        (1,3,((2,2,6),)),
         (1,5,((5,2,4),)),
         (1,6,((4,5,6),)),
         (1,7,((2,7,6),(2,0,5,6))),
         (0,4,((7,5),)),
     ),
     (
-        (1,1,((1,5),)),
+        (1,1,((1,5,6),)),
         (1,7,((3,3,6),(7,3,6))),
         (0,4,((0,1),)),
     ),
@@ -921,22 +921,22 @@
     (
         (1,1,((4,5,5,6),)),
         (1,3,((7,0,6),)),
-        (1,4,((4,5,6),(5,5,3,4))),
+        (1,4,((4,5,6),(5,5,3,4,6))),
         (1,5,((6,2,4,6),)),
-        (1,6,((7,0,5),(6,5,3))),
+        (1,6,((7,0,5,6),(6,5,3))),
     ),
     (
         (1,2,((6,4,5,6),)),
         (1,5,((5,3,3,6),)),
         (1,6,((5,2),)),
-        (1,7,((6,1,3),)),
+        (1,7,((6,1,3,6),)),
         (0,4,((0,2),(5,5))),
     ),
     (
-        (1,1,((7,0),)),
+        (1,1,((7,0,6),)),
         (1,2,((5,3,6),)),
-        (1,4,((7,5,3,4),)),
-        (1,7,((7,6,4),)),
+        (1,4,((7,5,3,4,6),)),
+        (1,7,((7,6,4,6),)),
     ),
     (
         (1,7,((1,3,6),)),
@@ -953,7 +953,7 @@
     ),
     (
         (1,1,((5,7,6),)),
-        (1,2,((7,6),)),
+        (1,2,((7,6,6),)),
         (1,5,((7,3,3),(3,4,6))),
         (1,7,((6,3,6),)),
         (0,4,((0,5),)),
@@ -963,7 +963,7 @@
         (1,7,((1,7,4,6),(5,3,5))),
     ),
     (
-        (1,2,((1,5),(5,5,3,5,6))),
+        (1,2,((1,5,6),(5,5,3,5,6))),
         (1,3,((5,2,5),)),
         (1,4,((7,6,6),)),
     ),
@@ -972,7 +972,7 @@
         (1,2,((7,5,5,6),)),
         (1,3,((2,0,6),)),
         (1,4,((5,7,6),(5,2,6))),
-        (1,6,((6,7),)),
+        (1,6,((6,7,6),)),
     ),
     (
         (1,2,((1,7,6),)),
@@ -982,13 +982,13 @@
     (
         (1,2,((7,0,6),)),
         (1,4,((1,7,6),)),
-        (1,7,((6,5),)),
+        (1,7,((6,5,6),)),
     ),
     (
         (1,1,((7,3,6),)),
         (1,3,((2,7,6),)),
-        (1,4,((6,1),)),
-        (1,5,((7,6),(4,5,6))),
+        (1,4,((6,1,6),)),
+        (1,5,((7,6,6),(4,5,6))),
     ),
     (
         (1,4,((6,2,6),)),
@@ -997,7 +997,7 @@
         (1,7,((5,5,6),)),
     ),
     (
-        (1,6,((7,6),)),
+        (1,6,((7,6,6),)),
         (1,7,((7,5,6),)),
     ),
     (

time: 71 us -> 72 us (1.014); the launches traced: 70.7 us -> 70.7 us
  no operation moved by 1% of the time
where the time goes in v5:
time: 72 us; the launch traced here: 70.7 us
  Pallas kernels  70.5 us (98%)
    pallas_call x1, Pallas kernels, gather(): pl.pallas_call(gather_kernel, out_shape=(pltpu.VMEM((8 * reads, bins), we...  55.4 us
    pallas_call x1, Pallas kernels, product(): pl.pallas_call(kernel, out_shape=jax.ShapeDtypeStruct((rows, cols), left....  15.1 us

profile of v5, /device:TPU:7, one launch (start us, length us, event | category | flops | bytes accessed | tf_op | source)
XLA Modules:
  0.0 70.7 jit_solution(8107254121720163630)
XLA Ops:
  0.0 55.4 %gather.1 = (bf16[2048,1024]{1,0:T(8,128)(2,1)S(1)}, bf16[4096,1024]{1,0:T(8,128)(2,1)S(1)}) custom-call(s32[1,2]{1,0:T(1,128)} %pattern_hbm.1, bf16[256,1024]{1,0:T(8,128)(2,1)} %weights_hbm.1), custom_call_target="tpu_custom_call" | custom-call | tf_op jit(solution)/shard_map/gather/pallas_call | solution.py:1200
  55.4 15.1 %product.1 = bf16[2048,4096]{1,0:T(8,128)(2,1)} custom-call(bf16[2048,1024]{1,0:T(8,128)(2,1)S(1)} %get-tuple-element.7.refs_0_, bf16[4096,1024]{1,0:T(8,128)(2,1)S(1)} %get-tuple-element.8.refs_1_), custom_call_target="tpu_custom_call" | custom-call | tf_op jit(solution)/shard_map/product/pallas_call | solution.py:1287
